TPU v7x, 256 devices: a whole 4x4x8 slice. The times are simulated.
256 devices in a mesh: lat: 64 (over z, y, x_lo), ch: 4 (over x_hi, core).
Axes of the slice: x: 4 (x_hi: 2, x_lo: 2; x = x_hi * 2 + x_lo), y: 4, z: 8, core: 2. Of those that a mesh axis runs over, the one named last changes fastest.
Arguments:
- output_gradient: bfloat16 [256, 900, 256], P('lat', None, 'ch'), may hold values from -6 to 6
- conv_in: bfloat16 [256, 900, 768], P('lat', None, 'ch'), may hold values from -6 to 6
- conv_weight: bfloat16 [3, 3, 768, 256], P(None, None, 'ch'), may hold values from -0.078125 to 0.078125
- modes: bfloat16 [448, 256, 8, 2, 96], P('lat', None, 'ch'), may hold values from -6 to 6
- w1: bfloat16 [8, 2, 96, 96], P('ch'), may hold values from -0.4375 to 0.4375
- b1: bfloat16 [8, 2, 96], P('ch'), may hold values from -6 to 6
- w2: bfloat16 [8, 2, 96, 96], P('ch'), may hold values from -0.4375 to 0.4375
Outputs:
- grad_in: bfloat16 [256, 900, 768], P('lat', None, 'ch')
- grad_conv: float32 [3, 3, 768, 256], P(None, None, 'ch')
- grad_w1: float32 [8, 2, 96, 96], P('ch')
- grad_b1: float32 [8, 2, 96], P('ch')
- grad_w2: float32 [8, 2, 96, 96], P('ch')
- grad_b2: float32 [8, 2, 96], P('ch')
All inputs are finite; a program needn't handle non-finite values.
Results may differ from a plain program's by a relative error of at most 0.012.
Values may be sent and summed in bfloat16 or wider, within the bound.
A program may use at most 128 MiB of HBM per device.

v0:
```python
import math

import jax
import jax.numpy as jnp
from jax import lax
from jax.sharding import PartitionSpec as P

DILATION_STEP = 4


def with_halo(cells, sides, width):
    for axis, dim in sides:
        count = lax.axis_size(axis)
        ends = count - 1
        head = lax.slice_in_dim(cells, 0, width, axis=dim)
        tail = lax.slice_in_dim(cells, cells.shape[dim] - width, cells.shape[dim], axis=dim)
        cells = jnp.concatenate(
            [
                lax.ppermute(tail, axis, [(i, (i + 1) % count) for i in range(ends)]),
                cells,
                lax.ppermute(head, axis, [((i + 1) % count, i) for i in range(ends)]),
            ],
            axis=dim,
        )
    return cells


def smooth_gate(values):
    return jax.nn.gelu(values, approximate=True)


def analysis_table(lon_count, mode_count):
    positions = jnp.arange(lon_count, dtype=jnp.int32)[:, None]
    wavenums = jnp.arange(mode_count, dtype=jnp.int32)[None, :]
    angle_index = positions * wavenums % lon_count
    angles = angle_index.astype(jnp.float32) * (2.0 * math.pi / lon_count)
    weights = jnp.where(wavenums == 0, 1.0, 2.0).astype(jnp.float32) / math.sqrt(lon_count)
    return jnp.stack([weights * jnp.cos(angles), -weights * jnp.sin(angles)], axis=1).astype(
        jnp.bfloat16
    )


def synthesis_table(lon_count, mode_count):
    wavenums = jnp.arange(mode_count, dtype=jnp.int32)[:, None]
    positions = jnp.arange(lon_count, dtype=jnp.int32)[None, :]
    angle_index = positions * wavenums % lon_count
    angles = angle_index.astype(jnp.float32) * (2.0 * math.pi / lon_count)
    factor = 1.0 / math.sqrt(lon_count)
    return jnp.stack([factor * jnp.cos(angles), -factor * jnp.sin(angles)], axis=0).astype(
        jnp.bfloat16
    )


def lat_tables(lat_count):
    wavenums = jnp.arange(lat_count, dtype=jnp.int32)[:, None]
    positions = jnp.arange(lat_count, dtype=jnp.int32)[None, :]
    angle_index = wavenums * positions % lat_count
    angles = angle_index.astype(jnp.float32) * (2.0 * math.pi / lat_count)
    cosine = jnp.cos(angles) / math.sqrt(lat_count)
    sine = jnp.sin(angles) / math.sqrt(lat_count)
    forward = jnp.stack(
        [jnp.stack([cosine, sine], axis=-1), jnp.stack([-sine, cosine], axis=-1)], axis=1
    )
    cos_t = cosine.T
    sin_t = sine.T
    inverse = jnp.stack(
        [jnp.stack([cos_t, -sin_t], axis=-1), jnp.stack([sin_t, cos_t], axis=-1)], axis=1
    )
    return (forward.astype(jnp.bfloat16), inverse.astype(jnp.bfloat16))


def complex_matrix(weight):
    real_part = weight[:, 0]
    imag_part = weight[:, 1]
    upper = jnp.concatenate([real_part, imag_part], axis=2)
    lower = jnp.concatenate([-imag_part, real_part], axis=2)
    return jnp.concatenate([upper, lower], axis=1)


def collapse(gradient, block_size):
    upper_left = gradient[:, :block_size, :block_size]
    upper_right = gradient[:, :block_size, block_size:]
    lower_left = gradient[:, block_size:, :block_size]
    lower_right = gradient[:, block_size:, block_size:]
    return jnp.stack([upper_left + lower_right, upper_right - lower_left], axis=1)


def block_backward(mode_vals, spec_vals, w1, b1, w2):
    block_size = w1.shape[-1]
    first = complex_matrix(w1)
    second = complex_matrix(w2)
    bias = b1.reshape(b1.shape[0], 2 * block_size).astype(jnp.float32)
    pre_act = (
        jnp.einsum("mbi,bij->mbj", mode_vals, first, preferred_element_type=jnp.float32) + bias
    )
    activated, slope = jax.vjp(smooth_gate, pre_act)
    act_half = activated.astype(jnp.bfloat16)
    d_act = jnp.einsum("mbj,bij->mbi", spec_vals, second, preferred_element_type=jnp.float32)
    d_pre = slope(d_act)[0].astype(jnp.bfloat16)
    d_modes = jnp.einsum("mbj,bij->mbi", d_pre, first, preferred_element_type=jnp.float32).astype(
        jnp.bfloat16
    )
    grad_second = collapse(
        jnp.einsum("mbi,mbj->bij", act_half, spec_vals, preferred_element_type=jnp.float32),
        block_size,
    )
    grad_first = collapse(
        jnp.einsum("mbi,mbj->bij", mode_vals, d_pre, preferred_element_type=jnp.float32), block_size
    )
    bias_second = jnp.sum(spec_vals, axis=0, dtype=jnp.float32).reshape(-1, 2, block_size)
    bias_first = jnp.sum(d_pre, axis=0, dtype=jnp.float32).reshape(-1, 2, block_size)
    return (d_modes, grad_first, bias_first, grad_second, bias_second)


def on_device(output_gradient, conv_in, conv_weight, modes, w1, b1, w2):
    row_count, lon_count, channels = conv_in.shape
    kx_local, lat_total, block_count, pair_count, block_size = modes.shape
    kx_total = kx_local * lax.axis_size("lat")
    out_total = conv_weight.shape[3]
    output_gathered = lax.all_gather(output_gradient, "ch", axis=2, tiled=True)
    padded_gradient = with_halo(output_gathered, (("lat", 0),), DILATION_STEP)
    conv_grad = jnp.zeros((row_count, lon_count, channels), jnp.float32)
    flat_in = conv_in.reshape(row_count * lon_count, channels)
    kernel_terms = []
    for row_offset in range(3):
        start_offset = DILATION_STEP - DILATION_STEP * (row_offset - 1)
        window_strip = padded_gradient[start_offset : start_offset + row_count]
        for column_offset in range(3):
            shifted_window = jnp.roll(window_strip, DILATION_STEP * (column_offset - 1), axis=1)
            flat_tap = shifted_window.reshape(row_count * lon_count, out_total)
            conv_grad = conv_grad + jnp.dot(
                flat_tap,
                conv_weight[row_offset, column_offset].T,
                preferred_element_type=jnp.float32,
            ).reshape(row_count, lon_count, channels)
            kernel_terms.append(jnp.dot(flat_in.T, flat_tap, preferred_element_type=jnp.float32))
    kernel_local = jnp.stack(kernel_terms).reshape(3, 3, channels, out_total)
    grad_conv = lax.psum(kernel_local, "lat")
    half_grad = conv_grad.astype(jnp.bfloat16)
    lon_table = analysis_table(lon_count, kx_total)
    lon_modes = jnp.einsum(
        "pqc,qik->pikc", half_grad, lon_table, preferred_element_type=jnp.float32
    ).astype(jnp.bfloat16)
    lon_modes = lon_modes.reshape(row_count, 2, kx_total, block_count, block_size)
    all_rows = lax.all_to_all(lon_modes, "lat", split_axis=2, concat_axis=0, tiled=True)
    lat_forward, lat_inverse = lat_tables(lat_total)
    spec_grad = jnp.einsum(
        "yopi,pikbs->kybos", lat_forward, all_rows, preferred_element_type=jnp.float32
    ).astype(jnp.bfloat16)
    spec_rows = spec_grad.reshape(kx_local * lat_total, block_count, 2 * block_size)
    mode_rows = modes.reshape(kx_local * lat_total, block_count, 2 * block_size)
    d_modes, first_local, first_bias, second_local, second_bias = block_backward(
        mode_rows, spec_rows, w1, b1, w2
    )
    d_modes = d_modes.reshape(kx_local, lat_total, block_count, 2, block_size)
    back_modes = jnp.einsum(
        "poyi,kybis->pokbs", lat_inverse, d_modes, preferred_element_type=jnp.float32
    ).astype(jnp.bfloat16)
    own_rows = lax.all_to_all(back_modes, "lat", split_axis=0, concat_axis=2, tiled=True)
    own_rows = own_rows.reshape(row_count, 2, kx_total, channels)
    syn_table = synthesis_table(lon_count, kx_total)
    spectral_part = jnp.einsum(
        "pikc,ikq->pqc", own_rows, syn_table, preferred_element_type=jnp.float32
    )
    grad_in = (conv_grad + spectral_part).astype(jnp.bfloat16)
    grad_w1, grad_b1, grad_w2, grad_b2 = lax.psum(
        (first_local, first_bias, second_local, second_bias), "lat"
    )
    return (grad_in, grad_conv, grad_w1, grad_b1, grad_w2, grad_b2)


def solution(mesh):
    placed = (
        P("lat", None, "ch"),
        P("lat", None, "ch"),
        P(None, None, "ch", None),
        P("lat", None, "ch", None, None),
        P("ch", None, None, None),
        P("ch", None, None),
        P("ch", None, None, None),
    )
    return jax.shard_map(
        on_device,
        mesh=mesh,
        in_specs=placed,
        out_specs=(
            P("lat", None, "ch"),
            P(None, None, "ch", None),
            P("ch", None, None, None),
            P("ch", None, None),
            P("ch", None, None, None),
            P("ch", None, None),
        ),
        check_vma=False,
    )
```

profile of v0, /device:TPU:8, one launch (start us, length us, event | category | flops | bytes accessed | tf_op | source)
XLA Modules:
  0.0 879.4 jit_solution(5215319962114698520)
XLA Ops:
  20.0 3.4 fusion.1
  23.4 19.0 %all-gather.2.cloned.1.call-done = bf16[4,900,256]{1,0,2:T(4,128)(2,1)} async-done(((bf16[4,900,64]{1,0,2:T(4,128)(2,1)}), bf16[4,900,256]{1,0,2:T(4,128)(2,1)}) %all-gather.2.cloned.1.call-update) | async-done | bytes 1843216 | tf_op jit(solution)/shard_map/all_gather | solution.py:120
  42.5 5.6 copy.46
  48.1 2.4 collective-permute-start
  50.6 8.8 %multiply_convert_fusion.1 = (bf16[900,1,448]{0,2,1:T(8,128)(2,1)}, bf16[900,1,448]{0,2,1:T(8,128)(2,1)}) fusion(f32[448]{0:T(512)S(1)} %fusion.120, f32[448]{0:T(512)S(1)} %select_multiply_fusion), kind=kLoop, calls=%fused_computation.47 | loop fusion | flops 5241600 | bytes 1616384 | tf_op jit(solution)/shard_map/convert.10
  59.4 3.4 collective-permute-start.1
  62.8 6.3 fusion.149
  69.1 4.1 copy.99
  76.4 4.6 copy.96
  86.1 2.6 fusion.12
  88.7 4.6 collective-permute-done
  93.3 3.3 fusion.153
  98.0 34.0 %collective-permute-done.1 = bf16[4,900,256]{2,0,1:T(4,128)(2,1)S(1)} collective-permute-done((bf16[4,900,256]{2,0,1:T(4,128)(2,1)}, bf16[4,900,256]{2,0,1:T(4,128)(2,1)S(1)}, u32[]{:S(2)}, u32[]{:S(2)}) %collective-permute-start.1) | collective-permute-done | bytes 1843232 | tf_op jit(solution)/shard_map/ppermute | solution.py:19
  138.0 3.9 fusion.108
  141.9 7.2 add_add_fusion
  149.1 5.3 fusion.31
  154.4 6.1 copy.67
  160.5 15.3 %all-to-all-start = ((bf16[4,2,448,2,96]{4,3,1,0,2:T(2,128)(2,1)}), bf16[4,2,448,2,96]{4,3,1,0,2:T(2,128)(2,1)}, u32[]{:S(2)}, u32[]{:S(2)}) async-start(bf16[4,2,448,2,96]{4,3,1,0,2:T(2,128)(2,1)} %copy.67), calls=%async_computation | async-start | bytes 3670016 | tf_op jit(solution)/shard_map/all_to_all | solution.py:145
  178.1 2.8 fusion.55
  180.9 2.9 fusion.73
  195.4 24.7 %all-to-all-done = bf16[4,2,448,2,96]{4,3,1,0,2:T(2,128)(2,1)} async-done(((bf16[4,2,448,2,96]{4,3,1,0,2:T(2,128)(2,1)}), bf16[4,2,448,2,96]{4,3,1,0,2:T(2,128)(2,1)}, u32[]{:S(2)}, u32[]{:S(2)}) %all-to-all-start) | async-done | bytes 1376288 | tf_op jit(solution)/shard_map/all_to_all | solution.py:145
  220.1 2.4 copy.69
  224.7 2.6 reshape.352
  227.3 3.3 fusion.41
  231.5 2.5 convert_reduce_fusion.1
  235.9 2.4 reshape.354
  240.6 3.7 copy.75
  244.3 7.0 all-to-all-start.1
  256.0 8.6 multiply_convert_fusion.3
  264.7 172.0 %all-reduce = (f32[2,2,96]{2,1,0:T(2,128)}, f32[2,2,96]{2,1,0:T(2,128)}) all-reduce(f32[2,2,96]{2,1,0:T(2,128)S(1)} %reshape.357, f32[2,2,96]{2,1,0:T(2,128)S(1)} %get-tuple-element.57), channel_id=1, replica_groups=mesh['lat'=64,'ch'=4] {'lat'}, use_global_device_ids=true, to_apply=%region_3.4 | all-reduce | flops 768 | bytes 6144 | tf_op jit(solution)/shard_map/psum | solution.py:166
  436.7 420.6 %all-reduce.4.cloned.1.call-done = (f32[3,3,192,256]{3,2,1,0:T(8,128)}, f32[2,2,96,96]{2,3,0,1:T(8,128)}, f32[2,2,96,96]{3,2,0,1:T(8,128)}) async-done(((f32[3,3,192,256]{3,2,1,0:T(8,128)}, f32[2,2,96,96]{2,3,0,1:T(8,128)}, f32[2,2,96,96]{3,2,0,1:T(8,128)}), (f32[3,3,192,256]{3,2,1,0:T(8,128)}, f32[2,2,96,96]{2,3,0,1:T(8,128)}, f32[2,2,96,96]{3,2,0,1:T(8,128)})) %all-reduce.4.cloned.1.call-update) | async-done | bytes 2064400 | tf_op jit(solution)/shard_map/psum | solution.py:138
  865.0 6.1 fusion
  (125 shorter events, 63.0 us)
Async XLA Ops:
  7.2 170.9 %copy-start = (bf16[4,900,192]{1,2,0:T(8,128)(2,1)S(1)}, bf16[4,900,192]{1,2,0:T(8,128)(2,1)}, u32[]{:S(2)}) copy-start(bf16[4,900,192]{1,2,0:T(8,128)(2,1)} %param.8) | copy-start | bytes 4147204
  7.2 35.3 %all-gather.2.cloned.1.call-start = ((), (), s32[]{:S(2)}) async-start(), calls=%async_computation.2 | async-start | bytes 2621440 | tf_op jit(solution)/shard_map/all_gather | solution.py:120
  12.8 2.4 copy-start.30
  12.8 5.9 copy-start.25
  48.1 45.2 %collective-permute-start = (bf16[4,900,256]{2,0,1:T(4,128)(2,1)}, bf16[4,900,256]{2,0,1:T(4,128)(2,1)}, u32[]{:S(2)}, u32[]{:S(2)}) collective-permute-start(bf16[4,900,256]{2,0,1:T(4,128)(2,1)} %copy.46), channel_id=1, source_target_pairs={{4,0},{8,4},{12,8},{16,12},{20,16},{24,20},{28,24},{32,28},{36,32}... | collective-permute-start | bytes 5529608 | tf_op jit(solution)/shard_map/ppermute | solution.py:21
  59.4 72.6 %collective-permute-start.1 = (bf16[4,900,256]{2,0,1:T(4,128)(2,1)}, bf16[4,900,256]{2,0,1:T(4,128)(2,1)S(1)}, u32[]{:S(2)}, u32[]{:S(2)}) collective-permute-start(bf16[4,900,256]{2,0,1:T(4,128)(2,1)} %copy.46), channel_id=1, source_target_pairs={{0,4},{4,8},{8,12},{12,16},{16,20},{20,24},{24,28},{28,32},{32,36}... | collective-permute-start | bytes 5529608 | tf_op jit(solution)/shard_map/ppermute | solution.py:19
  82.1 2.4 copy-start.4
  82.1 2.4 copy-start.17
  96.9 38.0 %copy-start.6 = (bf16[4,896,256]{2,1,0:T(8,128)(2,1)}, bf16[4,896,256]{2,1,0:T(8,128)(2,1)S(1)}, u32[]{:S(2)}) copy-start(bf16[4,896,256]{2,1,0:T(8,128)(2,1)S(1)} %copy.132) | copy-start | bytes 5505028
  98.0 37.7 %copy-start.10 = (bf16[4,896,256]{2,1,0:T(8,128)(2,1)}, bf16[4,896,256]{2,1,0:T(8,128)(2,1)S(1)}, u32[]{:S(2)}) copy-start(bf16[4,896,256]{2,1,0:T(8,128)(2,1)S(1)} %copy.135) | copy-start | bytes 5505028
  98.0 37.7 %copy-start.29 = (bf16[4,4,256]{2,1,0:T(4,128)(2,1)}, bf16[4,4,256]{2,1,0:T(4,128)(2,1)S(1)}, u32[]{:S(2)}) copy-start(bf16[4,4,256]{2,1,0:T(4,128)(2,1)S(1)} %copy.134) | copy-start | bytes 24580
  133.2 3.3 copy-start.8
  141.9 7.2 copy-start.16
  160.5 59.6 %all-to-all-start = ((bf16[4,2,448,2,96]{4,3,1,0,2:T(2,128)(2,1)}), bf16[4,2,448,2,96]{4,3,1,0,2:T(2,128)(2,1)}, u32[]{:S(2)}, u32[]{:S(2)}) async-start(bf16[4,2,448,2,96]{4,3,1,0,2:T(2,128)(2,1)} %copy.67), calls=%async_computation | async-start | bytes 3670016 | tf_op jit(solution)/shard_map/all_to_all | solution.py:145
  180.9 2.9 copy-start.7
  183.8 1.7 copy-start.5
  187.1 2.1 copy-start.3
  189.2 1.7 copy-start.9
  195.4 27.1 %copy-start.23 = (bf16[256,1,256,2]{2,0,3,1:T(8,128)(2,1)S(1)}, bf16[256,1,256,2]{2,0,3,1:T(8,128)(2,1)}, u32[]{:S(2)}) copy-start(bf16[256,1,256,2]{2,0,3,1:T(8,128)(2,1)} %get-tuple-element.46) | copy-start | bytes 786436
  195.4 27.1 %copy-start.24 = (bf16[256,1,256,2]{2,0,3,1:T(8,128)(2,1)S(1)}, bf16[256,1,256,2]{2,0,3,1:T(8,128)(2,1)}, u32[]{:S(2)}) copy-start(bf16[256,1,256,2]{2,0,3,1:T(8,128)(2,1)} %get-tuple-element.49) | copy-start | bytes 786436
  227.3 4.2 copy-start.12
  227.3 4.2 copy-start.15
  227.3 4.2 copy-start.26
  227.3 4.2 copy-start.27
  227.3 4.2 copy-start.28
  231.5 3.7 copy-start.19
  235.8 2.4 copy-start.21
  235.8 2.4 copy-start.22
  244.3 7.0 copy-start.20
  244.3 616.4 %all-to-all-start.1 = ((bf16[256,2,7,2,96]{4,3,2,1,0:T(2,128)(2,1)}), bf16[256,2,7,2,96]{4,3,2,1,0:T(2,128)(2,1)S(1)}, u32[]{:S(2)}, u32[]{:S(2)}) async-start(bf16[256,2,7,2,96]{4,3,2,1,0:T(2,128)(2,1)} %copy.75), calls=%async_computation.1 | async-start | bytes 3670016 | tf_op jit(solution)/shard_map/all_to_all | solution.py:159
  251.2 606.1 %all-reduce.4.cloned.1.call-start = ((), (), s32[]{:S(2)}) async-start(), calls=%async_computation.3 | async-start | bytes 4325376 | tf_op jit(solution)/shard_map/psum | solution.py:138
  865.0 6.1 copy-start.13
  (5 other events, 7.2 us)
Sparse Core Ops, SparseCore 0:
  10.4 32.0 all-gather.1
  256.1 601.1 all-reduce.3
where the time goes:
time: 888 us; the launch traced here: 879 us
  waiting for transfers between devices  503 us (57%)
  blocking collectives  172 us (19%)
  local copies, waits for them, and re-layouts  70.7 us (8%)
  matrix products  63.9 us (7%)
  starting transfers between devices  28.1 us (3%)
  other arithmetic  26.9 us (3%)
  between operations  14.8 us (2%)
    psum x1, waiting for transfers between devices, on_device(): grad_conv = lax.psum(kernel_local, 'lat')  421 us
    psum x1, blocking collectives, on_device(): lax.psum((first_local, first_bias, second_local, second_bias), 'lat')  172 us
    ppermute x1, waiting for transfers between devices, with_halo(): lax.ppermute(tail, axis, [(i, (i + 1) % count) for i in range(ends)])  34 us
    unnamed x81, local copies, waits for them, and re-layouts  25.3 us
    all_to_all x1, waiting for transfers between devices, on_device(): lax.all_to_all(lon_modes, 'lat', split_axis=2, concat_axis=0, tiled=True)  24.7 us
    another operation x4, other arithmetic  20.8 us
    dot_general x9, matrix products, on_device(): jnp.dot(flat_tap, conv_weight[row_offset, column_offset].T, preferred_ele...  19.8 us
    all_gather x1, waiting for transfers between devices, on_device(): output_gathered = lax.all_gather(output_gradient, 'ch', axis=2, tiled=True)  19 us
  transfers between devices with their start and end apart: 6, of which 5 were waited for; matrix products, arithmetic and copies ran while one was open for 10% of the time, Pallas kernels for 0%

commit v1 on v0

v1 whole, which is shorter than its diff:
```python
import functools
import math

import jax
import jax.numpy as jnp
import ml_dtypes
import numpy as np
from jax import lax
from jax.experimental import pallas as pl
from jax.experimental.pallas import tpu as pltpu
from jax.sharding import PartitionSpec as P

MESH = pl.DeviceIdType.MESH
F32, BF16 = jnp.float32, jnp.bfloat16
STEP = 4
LON, PAD = 900, 1024
NLAT = 64
ROWS = 4
NK = 7
KX = 448
CI, CO = 192, 256
PC = ROWS * CI
VMEM = 56 * 1024 * 1024
NT = (((1,), (1,)), ((), ()))
TN = (((0,), (0,)), ((), ()))
NN = (((1,), (0,)), ((), ()))


def dot(a, b, dims=NN):
    return lax.dot_general(a, b, dims, preferred_element_type=F32)


def lon_tables():
    q = np.arange(LON)[None, :]
    d, i, kk = np.meshgrid(np.arange(NLAT), np.arange(2), np.arange(8), indexing="ij")
    k = (d * NK + kk).reshape(-1, 1)
    i = i.reshape(-1, 1)
    live = (kk.reshape(-1, 1) < NK).astype(np.float64)
    angle = (k * q % LON) * (2.0 * math.pi / LON)
    base = np.where(i == 0, np.cos(angle), -np.sin(angle)) / math.sqrt(LON) * live
    weight = np.where(k == 0, 1.0, 2.0)
    pad = ((0, 0), (0, PAD - LON))
    ana = np.pad(base * weight, pad).astype(ml_dtypes.bfloat16)
    syn = np.pad(base, pad).astype(ml_dtypes.bfloat16)
    return ana, syn


def lat_tables():
    y = np.arange(NLAT)[:, None]
    l = np.arange(NLAT)[None, :]
    angle = (y * l % NLAT) * (2.0 * math.pi / NLAT)
    c, s = np.cos(angle) / 16.0, np.sin(angle) / 16.0
    small = np.array([[c, s], [-s, c]])
    fwd = np.zeros((NK, 2, NLAT, NLAT, 2, 8))
    for k in range(NK):
        fwd[k, :, :, :, :, k] = small.transpose(0, 2, 3, 1)
    fwd = fwd.reshape(NK, 2 * NLAT, 16 * NLAT)
    back = np.array([[c, -s], [s, c]])
    inv = np.zeros((NLAT, 2, 8, NK, 2, NLAT))
    for k in range(NK):
        inv[:, :, k, k] = back.transpose(3, 0, 1, 2)
    inv = inv.reshape(16 * NLAT, NK * 2 * NLAT)
    tw = np.zeros((2, ROWS, NLAT, 1))
    for p in range(ROWS):
        a = np.arange(NLAT) * p * (2.0 * math.pi / 256)
        tw[0, p, :, 0], tw[1, p, :, 0] = np.cos(a), np.sin(a)
    tw = np.broadcast_to(tw, (2, ROWS, NLAT, CI))
    return (
        fwd.astype(ml_dtypes.bfloat16),
        inv.astype(ml_dtypes.bfloat16),
        np.ascontiguousarray(tw).astype(np.float32),
    )


def gather_kernel(g_ref, out_ref, send, recv, local):
    me = lax.axis_index("lat")
    ch = lax.axis_index("ch")
    xlo = lax.rem(me, 2)
    near = 2 * xlo
    far = 2 - near
    pair = me + 1 - 2 * xlo
    ch2 = lax.rem(ch + 2, 4)
    core = ch + 1 - 2 * lax.rem(ch, 2)
    nxt = lax.rem(me + 2 - 4 * xlo + NLAT, NLAT)
    prv = lax.rem(me - 2 + 4 * xlo + NLAT, NLAT)

    barrier = pltpu.get_barrier_semaphore()
    for dev in ((pair, ch), (pair, ch2), (me, core), (nxt, ch), (prv, ch)):
        pl.semaphore_signal(barrier, inc=1, device_id=dev, device_id_type=MESH)
    pl.semaphore_wait(barrier, 5)

    def rows(c):
        return pl.ds(pl.multiple_of(c * 64, 64), 64)

    def at(p, slot, c):
        return out_ref.at[p, slot, rows(c), :]

    started = []

    def go(src, dst, kind, p, dev):
        copy = pltpu.make_async_remote_copy(
            src_ref=src,
            dst_ref=dst,
            send_sem=send.at[kind, p],
            recv_sem=recv.at[kind, p],
            device_id=dev,
            device_id_type=MESH,
        )
        copy.start()
        started.append(copy)

    def got(kind, p, dst):
        pltpu.make_async_remote_copy(
            src_ref=dst,
            dst_ref=dst,
            send_sem=send.at[kind, p],
            recv_sem=recv.at[kind, p],
            device_id=(me, core),
            device_id_type=MESH,
        ).wait_recv()

    own = pltpu.make_async_copy(g_ref, out_ref.at[:, 1, rows(ch), :], local)
    own.start()
    for p in range(ROWS):
        go(g_ref.at[p], at(p, far, ch), 0, p, (pair, ch))
        go(g_ref.at[p], at(p, far, ch), 1, p, (pair, ch2))
    for p in range(ROWS):
        go(g_ref.at[p], at(p, 1, ch), 5, p, (me, core))
    for p in range(ROWS):
        got(0, p, at(p, near, ch))
        go(at(p, near, ch), at(p, far, ch), 3, p, (nxt, ch))
        if p < 2:
            go(at(p, near, ch), at(p, 1, ch), 2, p, (pair, ch2))
        go(at(p, near, ch), at(p, near, ch), 6, p, (me, core))
        got(1, p, at(p, near, ch2))
        go(at(p, near, ch2), at(p, far, ch2), 4, p, (nxt, ch))
        if p >= 2:
            go(at(p, near, ch2), at(p, 1, ch2), 2, p, (pair, ch))
        go(at(p, near, ch2), at(p, near, ch2), 7, p, (me, core))
    for p in range(ROWS):
        got(2, p, at(p, 1, ch2))
        go(at(p, 1, ch2), at(p, 1, ch2), 8, p, (me, core))
        got(3, p, at(p, far, ch))
        go(at(p, far, ch), at(p, far, ch), 9, p, (me, core))
        got(4, p, at(p, far, ch2))
        go(at(p, far, ch2), at(p, far, ch2), 10, p, (me, core))
    core2 = lax.rem(core + 2, 4)
    for p in range(ROWS):
        got(5, p, at(p, 1, core))
        got(6, p, at(p, near, core))
        got(7, p, at(p, near, core2))
        got(8, p, at(p, 1, core2))
        got(9, p, at(p, far, core))
        got(10, p, at(p, far, core2))
    own.wait()
    for copy in started:
        copy.wait_send()

    @pl.when(me == 0)
    def _():
        out_ref[:, 2] = jnp.zeros((ROWS, CO, PAD), BF16)

    @pl.when(me == NLAT - 1)
    def _():
        out_ref[:, 0] = jnp.zeros((ROWS, CO, PAD), BF16)


def gather(g):
    return pl.pallas_call(
        gather_kernel,
        out_shape=jax.ShapeDtypeStruct((ROWS, 3, CO, PAD), BF16),
        in_specs=[pl.BlockSpec(memory_space=pltpu.VMEM)],
        out_specs=pl.BlockSpec(memory_space=pltpu.VMEM),
        scratch_shapes=[
            pltpu.SemaphoreType.DMA((11, ROWS)),
            pltpu.SemaphoreType.DMA((11, ROWS)),
            pltpu.SemaphoreType.DMA,
        ],
        compiler_params=pltpu.CompilerParams(
            collective_id=0, has_side_effects=True, vmem_limit_bytes=VMEM
        ),
        name="gather_rows",
    )(g)


def shifted(x, s):
    if s == 0:
        return x
    lane = lax.broadcasted_iota(jnp.int32, x.shape, 1)
    if s > 0:
        return jnp.where(lane < s, pltpu.roll(x, PAD - LON + s, 1), pltpu.roll(x, s, 1))
    return jnp.where(lane >= LON + s, pltpu.roll(x, LON + s, 1), pltpu.roll(x, PAD + s, 1))


def conv_kernel(g_ref, ci_ref, w_ref, ana_ref, cg_ref, a_ref, q_ref, hg_ref, acc_ref, cib_ref):
    acc_ref[...] = jnp.zeros_like(acc_ref)

    def row(p, carry):
        g = g_ref[p].reshape(3 * CO, PAD)
        total = jnp.zeros((CI, PAD), F32)
        for b in range(3):
            part = dot(w_ref[b * CI : (b + 1) * CI, :], g)
            total = total + shifted(part, STEP * (b - 1))
        at = pl.ds(pl.multiple_of(p * CI, CI), CI)
        cg_ref[at, :] = total
        hg_ref[at, :] = total.astype(BF16)
        x = jnp.concatenate(
            [ci_ref[p].astype(F32), jnp.zeros((CI, PAD - LON), F32)], axis=1
        )
        for b in range(3):
            cib_ref[b * CI : (b + 1) * CI, :] = shifted(x, -STEP * (b - 1)).astype(BF16)
        for m in range(3):
            acc_ref[m * CI : (m + 1) * CI, :] += dot(cib_ref[m * CI : (m + 1) * CI, :], g, NT)
        return carry

    lax.fori_loop(0, ROWS, row, 0)

    def chunk(m, carry):
        at = pl.ds(pl.multiple_of(m * 128, 128), 128)
        a_ref[at, :] = dot(ana_ref[at, :], hg_ref[...], NT).astype(BF16)
        return carry

    lax.fori_loop(0, 8, chunk, 0)
    for rr in range(4):
        for cc in range(2):
            for t in range(3):
                col = cc * 384 + t * 128
                q_ref[rr * 2 + cc, t * 144 : (t + 1) * 144, :] = acc_ref[
                    rr * 144 : (rr + 1) * 144, col : col + 128
                ].astype(BF16)


def local_call(kernel, outs, scratch, name, flops):
    def call(*args):
        n_out = len(outs)
        return pl.pallas_call(
            kernel,
            out_shape=[jax.ShapeDtypeStruct(s, t) for s, t in outs],
            in_specs=[pl.BlockSpec(memory_space=pltpu.VMEM)] * len(args),
            out_specs=[pl.BlockSpec(memory_space=pltpu.VMEM)] * n_out,
            scratch_shapes=scratch,
            compiler_params=pltpu.CompilerParams(vmem_limit_bytes=VMEM),
            cost_estimate=pl.CostEstimate(flops=flops, bytes_accessed=8 << 20, transcendentals=0),
            name=name,
        )(*args)

    return call


def greet_all(me):
    barrier = pltpu.get_barrier_semaphore()

    def hello(o, carry):
        dev = {"lat": lax.rem(me + o, NLAT)}
        pl.semaphore_signal(barrier, inc=1, device_id=dev, device_id_type=MESH)
        return carry

    lax.fori_loop(1, NLAT, hello, 0)
    pl.semaphore_wait(barrier, NLAT - 1)


def swap_copy(a_ref, r_ref, send, recv, me, o):
    to = lax.rem(me + o, NLAT)
    return pltpu.make_async_remote_copy(
        src_ref=a_ref.at[to],
        dst_ref=r_ref.at[me],
        send_sem=send.at[o],
        recv_sem=recv.at[o],
        device_id={"lat": to},
        device_id_type=MESH,
    )


def swap_start(a_ref, r_ref, send, recv, local, me):
    pltpu.make_async_copy(a_ref.at[me], r_ref.at[me], local).start()

    def go(j, carry):
        swap_copy(a_ref, r_ref, send, recv, me, j).start()
        swap_copy(a_ref, r_ref, send, recv, me, NLAT - j).start()
        return carry

    lax.fori_loop(1, NLAT // 2, go, 0)
    swap_copy(a_ref, r_ref, send, recv, me, NLAT // 2).start()


def swap_wait(a_ref, r_ref, send, recv, local, me):
    def done(o, carry):
        source = lax.rem(me - o + NLAT, NLAT)
        pltpu.make_async_remote_copy(
            src_ref=a_ref.at[lax.rem(me + o, NLAT)],
            dst_ref=r_ref.at[source],
            send_sem=send.at[o],
            recv_sem=recv.at[o],
            device_id={"lat": lax.rem(me + o, NLAT)},
            device_id_type=MESH,
        ).wait()
        return carry

    lax.fori_loop(1, NLAT, done, 0)
    pltpu.make_async_copy(a_ref.at[me], r_ref.at[me], local).wait()


def swap_kernel(a_ref, r_ref, send, recv, local):
    me = lax.axis_index("lat")
    greet_all(me)
    swap_start(a_ref, r_ref, send, recv, local, me)
    swap_wait(a_ref, r_ref, send, recv, local, me)


def swap(a):
    return pl.pallas_call(
        swap_kernel,
        out_shape=jax.ShapeDtypeStruct(a.shape, a.dtype),
        in_specs=[pl.BlockSpec(memory_space=pltpu.VMEM)],
        out_specs=pl.BlockSpec(memory_space=pltpu.VMEM),
        scratch_shapes=[
            pltpu.SemaphoreType.DMA((NLAT,)),
            pltpu.SemaphoreType.DMA((NLAT,)),
            pltpu.SemaphoreType.DMA,
        ],
        compiler_params=pltpu.CompilerParams(
            collective_id=1, has_side_effects=True, vmem_limit_bytes=VMEM
        ),
        name="swap_modes",
    )(a)


ROOT = math.sqrt(2.0 / math.pi)


def filter_kernel(
    r_ref, u_ref, fwd_ref, inv_ref, tw_ref, m1_ref, m2_ref, b1_ref, out_ref, q_ref,
    e_ref, g1_ref, g2_ref, bias_ref,
):
    g1_ref[...] = jnp.zeros_like(g1_ref)
    g2_ref[...] = jnp.zeros_like(g2_ref)
    bias_ref[...] = jnp.zeros_like(bias_ref)

    def mode(k, carry):
        z = dot(fwd_ref[k], r_ref[...])
        wr, wi = [], []
        for p in range(ROWS):
            zr = z[:NLAT, p * CI : (p + 1) * CI]
            zi = z[NLAT:, p * CI : (p + 1) * CI]
            if p > 0:
                c, s = tw_ref[0, p], tw_ref[1, p]
                zr, zi = zr * c + zi * s, zi * c - zr * s
            wr.append(zr)
            wi.append(zi)
        ar, ai = wr[0] + wr[2], wi[0] + wi[2]
        br, bi = wr[0] - wr[2], wi[0] - wi[2]
        cr, ci = wr[1] + wr[3], wi[1] + wi[3]
        dr, di = wr[1] - wr[3], wi[1] - wi[3]
        vr = jnp.concatenate([ar + cr, br + di, ar - cr, br - di], axis=0).astype(BF16)
        vi = jnp.concatenate([ai + ci, bi - dr, ai - ci, bi + dr], axis=0).astype(BF16)

        u = u_ref[k]
        pre = dot(u, m1_ref[...]) + b1_ref[...]
        sq = pre * pre
        th = jnp.tanh(ROOT * pre * (1.0 + 0.044715 * sq))
        act = (0.5 * pre * (1.0 + th)).astype(BF16)
        slope = 0.5 * (1.0 + th) + 0.5 * pre * (1.0 - th * th) * (
            ROOT * (1.0 + 3.0 * 0.044715 * sq)
        )
        d_act = dot(vr, m2_ref[0], NT) + dot(vi, m2_ref[1], NT)
        d_pre = (d_act * slope).astype(BF16)
        g2_ref[0] += dot(act, vr, TN)
        g2_ref[1] += dot(act, vi, TN)
        g1_ref[...] += dot(u, d_pre, TN)
        bias_ref[0:1, :] += jnp.sum(d_pre.astype(F32), axis=0, keepdims=True)
        bias_ref[1:2, 0:CI] += jnp.sum(vr.astype(F32), axis=0, keepdims=True)
        bias_ref[2:3, 0:CI] += jnp.sum(vi.astype(F32), axis=0, keepdims=True)
        xr = dot(d_pre, m1_ref[0:CI, :], NT).astype(BF16).astype(F32)
        xi = dot(d_pre, m1_ref[CI:, :], NT).astype(BF16).astype(F32)
        xr = [xr[j * NLAT : (j + 1) * NLAT] for j in range(4)]
        xi = [xi[j * NLAT : (j + 1) * NLAT] for j in range(4)]
        ar, ai = xr[0] + xr[2], xi[0] + xi[2]
        br, bi = xr[0] - xr[2], xi[0] - xi[2]
        cr, ci = xr[1] + xr[3], xi[1] + xi[3]
        dr, di = xr[1] - xr[3], xi[1] - xi[3]
        er = [ar + cr, br - di, ar - cr, br + di]
        ei = [ai + ci, bi + dr, ai - ci, bi - dr]
        for p in range(1, ROWS):
            c, s = tw_ref[0, p], tw_ref[1, p]
            er[p], ei[p] = er[p] * c - ei[p] * s, ei[p] * c + er[p] * s
        at = pl.multiple_of(k * 2 * NLAT, 2 * NLAT)
        e_ref[pl.ds(at, NLAT), :] = jnp.concatenate(er, axis=1).astype(BF16)
        e_ref[pl.ds(at + NLAT, NLAT), :] = jnp.concatenate(ei, axis=1).astype(BF16)
        return carry

    lax.fori_loop(0, NK, mode, 0)

    def chunk(m, carry):
        at = pl.ds(pl.multiple_of(m * 128, 128), 128)
        out_ref[at, :] = dot(inv_ref[at, :], e_ref[...]).astype(BF16)
        return carry

    lax.fori_loop(0, 8, chunk, 0)

    q_ref[...] = jnp.zeros_like(q_ref)
    g1 = g1_ref[...]
    h1 = (g1[:CI, :CI] + g1[CI:, CI:], g1[:CI, CI:] - g1[CI:, :CI])
    h2 = (g2_ref[0, :CI, :] + g2_ref[1, CI:, :], g2_ref[1, :CI, :] - g2_ref[0, CI:, :])
    bias = bias_ref[...]
    b1 = (bias[0:1, :CI], bias[0:1, CI:])
    b2 = (bias[1:2, :CI], bias[2:3, :CI])
    for w, (h, b) in enumerate(((h1, b1), (h2, b2))):
        for n in range(2):
            for part in range(2):
                j = w * 4 + n * 2 + part
                q_ref[j, 0:96, 0:96] = h[part][n * 96 : (n + 1) * 96, n * 96 : (n + 1) * 96].astype(BF16)
                tail = jnp.broadcast_to(b[part][:, n * 96 : (n + 1) * 96], (16, 96))
                q_ref[j, 96:112, 0:96] = tail.astype(BF16)


QC, QF, QR, QZ = 432, 112, 544, 80


def back_kernel(
    a_ref, qc_ref, qf_ref, r_ref, out_ref, in1, buf2, in2, buf4,
    send, recv, local, send1, recv1, send2, recv2, send3, recv3, send4, recv4, local4,
):
    me = lax.axis_index("lat")
    z, spot = me // 8, lax.rem(me, 8)
    greet_all(me)

    def plane(o):
        return z * 8 + lax.rem(spot + o, 8)

    def column(o):
        return lax.rem(z + o, 8) * 8 + spot

    def remote(src, dst, s, r, lat):
        return pltpu.make_async_remote_copy(
            src_ref=src, dst_ref=dst, send_sem=s, recv_sem=r,
            device_id={"lat": lat}, device_id_type=MESH,
        )

    def first(o, slot):
        peer = lax.rem(spot + o, 8)
        return (
            remote(qc_ref.at[peer], in1.at[slot, pl.ds(0, QC), :], send1.at[0, o], recv1.at[0, o], plane(o)),
            remote(qf_ref.at[peer], in1.at[slot, pl.ds(QC, QF), :], send1.at[1, o], recv1.at[1, o], plane(o)),
        )

    for o in range(1, 8):
        for copy in first(o, spot):
            copy.start()
    swap_start(a_ref, r_ref, send, recv, local, me)

    total_c = qc_ref[spot].astype(F32)
    total_f = qf_ref[spot].astype(F32)
    for o in range(1, 8):
        slot = lax.rem(spot - o + 8, 8)
        for copy in first(o, slot):
            copy.wait()
        total_c = total_c + in1[slot, 0:QC, :].astype(F32)
        total_f = total_f + in1[slot, QC:QR, :].astype(F32)
    buf2[0:QC, :] = total_c.astype(BF16)
    buf2[QC:QR, :] = total_f.astype(BF16)
    buf2[QR:, :] = jnp.zeros((8 * QZ - QR, 128), BF16)

    def zrows(i):
        return pl.ds(pl.multiple_of(i * QZ, 16), QZ)

    def second(o, slot):
        return remote(buf2.at[zrows(lax.rem(z + o, 8)), :], in2.at[slot], send2.at[o], recv2.at[o], column(o))

    for o in range(1, 8):
        second(o, z).start()
    total = buf2[zrows(z), :].astype(F32)
    for o in range(1, 8):
        slot = lax.rem(z - o + 8, 8)
        second(o, slot).wait()
        total = total + in2[slot].astype(F32)
    buf4[zrows(z), :] = total.astype(BF16)

    def third(o, slot):
        return remote(buf4.at[zrows(z), :], buf4.at[zrows(slot), :], send3.at[o], recv3.at[o], column(o))

    for o in range(1, 8):
        third(o, z).start()
    for o in range(1, 8):
        third(o, lax.rem(z - o + 8, 8)).wait()

    def fourth(o, slot):
        return remote(buf4.at[pl.ds(0, QR), :], out_ref.at[slot], send4.at[o], recv4.at[o], plane(o))

    own = pltpu.make_async_copy(buf4.at[pl.ds(0, QR), :], out_ref.at[spot], local4)
    own.start()
    for o in range(1, 8):
        fourth(o, spot).start()
    for o in range(1, 8):
        fourth(o, lax.rem(spot - o + 8, 8)).wait()
    own.wait()
    swap_wait(a_ref, r_ref, send, recv, local, me)


def back(a, qc, qf):
    dma = pltpu.SemaphoreType.DMA
    return pl.pallas_call(
        back_kernel,
        out_shape=[
            jax.ShapeDtypeStruct(a.shape, a.dtype),
            jax.ShapeDtypeStruct((8, QR, 128), BF16),
        ],
        in_specs=[pl.BlockSpec(memory_space=pltpu.VMEM)] * 3,
        out_specs=[pl.BlockSpec(memory_space=pltpu.VMEM)] * 2,
        scratch_shapes=[
            pltpu.VMEM((8, QR, 128), BF16),
            pltpu.VMEM((8 * QZ, 128), BF16),
            pltpu.VMEM((8, QZ, 128), BF16),
            pltpu.VMEM((8 * QZ, 128), BF16),
            dma((NLAT,)), dma((NLAT,)), dma,
            dma((2, 8)), dma((2, 8)), dma((8,)), dma((8,)),
            dma((8,)), dma((8,)), dma((8,)), dma((8,)), dma,
        ],
        compiler_params=pltpu.CompilerParams(
            collective_id=2, has_side_effects=True, vmem_limit_bytes=VMEM
        ),
        name="swap_back",
    )(a, qc, qf)


def synth_kernel(r_ref, syn_ref, cg_ref, q_ref, out_ref, gc_ref):
    for m in range(6):
        at = slice(m * 128, (m + 1) * 128)
        part = dot(r_ref[:, at], syn_ref[...], TN) + cg_ref[at, :]
        out_ref[at, :] = part[:, :LON].astype(BF16)
    for rr in range(4):
        for cc in range(2):
            for t in range(3):
                a, o = divmod(cc * 384 + t * 128, CO)
                r = rr * 144
                while r < (rr + 1) * 144:
                    b, c = divmod(r, CI)
                    n = min(CI - c, (rr + 1) * 144 - r)
                    at = t * 144 + r - rr * 144
                    gc_ref[a, b, c : c + n, o : o + 128] = q_ref[rr * 2 + cc, at : at + n, :].astype(F32)
                    r += n


def block_diag(w, part):
    zero = jnp.zeros_like(w[0, part])
    return jnp.concatenate(
        [
            jnp.concatenate([w[0, part], zero], axis=1),
            jnp.concatenate([zero, w[1, part]], axis=1),
        ],
        axis=0,
    )


def on_device(output_gradient, conv_in, conv_weight, modes, w1, b1, w2):
    ana, syn = lon_tables()
    fwd, inv, tw = lat_tables()
    g = jnp.pad(jnp.transpose(output_gradient, (0, 2, 1)), ((0, 0), (0, 0), (0, PAD - LON)))
    ci = jnp.transpose(conv_in, (0, 2, 1))
    w = jnp.transpose(conv_weight, (1, 2, 0, 3)).reshape(3 * CI, 3 * CO)
    u = jnp.transpose(modes, (0, 1, 3, 2, 4)).reshape(NK, 256, 2 * CI)
    p0, p1 = block_diag(w1, 0), block_diag(w1, 1)
    m1 = jnp.concatenate(
        [jnp.concatenate([p0, p1], axis=1), jnp.concatenate([-p1, p0], axis=1)], axis=0
    )
    p0, p1 = block_diag(w2, 0), block_diag(w2, 1)
    m2 = jnp.stack([jnp.concatenate([p0, -p1], axis=0), jnp.concatenate([p1, p0], axis=0)])
    bias = jnp.transpose(b1, (1, 0, 2)).reshape(1, 2 * CI).astype(F32)

    gathered = gather(g)
    cg, sent, qc = local_call(
        conv_kernel,
        [((PC, PAD), F32), ((16 * NLAT, PC), BF16), ((8, QC, 128), BF16)],
        [
            pltpu.VMEM((PC, PAD), BF16),
            pltpu.VMEM((3 * CI, 3 * CO), F32),
            pltpu.VMEM((3 * CI, PAD), BF16),
        ],
        "conv_terms",
        8_000_000_000,
    )(gathered, ci, w, ana)
    got = swap(sent.reshape(NLAT, 16, PC))
    sent_back, qf = local_call(
        filter_kernel,
        [((16 * NLAT, PC), BF16), ((8, QF, 128), BF16)],
        [
            pltpu.VMEM((NK * 2 * NLAT, PC), BF16),
            pltpu.VMEM((2 * CI, 2 * CI), F32),
            pltpu.VMEM((2, 2 * CI, CI), F32),
            pltpu.VMEM((8, 2 * CI), F32),
        ],
        "spectral_filter",
        6_000_000_000,
    )(got.reshape(16 * NLAT, PC), u, fwd, inv, tw, m1, m2, bias)
    own, sums = back(sent_back.reshape(NLAT, 16, PC), qc, qf)
    grad_in, grad_conv = local_call(
        synth_kernel,
        [((PC, LON), BF16), ((3, 3, CI, CO), F32)],
        [],
        "synthesis",
        1_600_000_000,
    )(own.reshape(16 * NLAT, PC), syn, cg, sums)
    grad_in = jnp.transpose(grad_in.reshape(ROWS, CI, LON), (0, 2, 1))
    small = sums[:, QC:, :96].astype(F32).reshape(2, 2, 2, QF, 96)
    grad_w, grad_b = small[:, :, :, :96], small[:, :, :, 96]
    return (grad_in, grad_conv, grad_w[0], grad_b[0], grad_w[1], grad_b[1])


def solution(mesh):
    placed = (
        P("lat", None, "ch"),
        P("lat", None, "ch"),
        P(None, None, "ch", None),
        P("lat", None, "ch", None, None),
        P("ch", None, None, None),
        P("ch", None, None),
        P("ch", None, None, None),
    )
    return jax.shard_map(
        on_device,
        mesh=mesh,
        in_specs=placed,
        out_specs=(
            P("lat", None, "ch"),
            P(None, None, "ch", None),
            P("ch", None, None, None),
            P("ch", None, None),
            P("ch", None, None, None),
            P("ch", None, None),
        ),
        check_vma=False,
    )
```

time: 888 us -> 216 us (0.24)
  waiting for transfers between devices: 503 us -> 0 us
  Pallas kernels: 0 us -> 203 us
  blocking collectives: 172 us -> 0 us
  matrix products: 63.9 us -> 0 us
  local copies, waits for them, and re-layouts: 70.7 us -> 8.91 us
  starting transfers between devices: 28.1 us -> 0 us
  other arithmetic: 26.9 us -> 1.77 us
  between operations: 14.8 us -> 0.81 us
    psum x1 -> x0, waiting for transfers between devices: 421 us -> none  [on_device(): grad_conv = lax.psum(kernel_local, 'lat')]
    pallas_call x0 -> x6, Pallas kernels: none -> 203 us  [the longest x1 69.9 us: back(): pl.pallas_call(back_kernel, out_shape=[jax.ShapeDtypeStruct(a.shape, a.dt...]
    psum x1 -> x0, blocking collectives: 172 us -> none  [on_device(): lax.psum((first_local, first_bias, second_local, second_bias), 'lat')]
    dot_general x27 -> x0, matrix products: 63.9 us -> none  [the longest x9 19.8 us: on_device(): jnp.dot(flat_tap, conv_weight[row_offset, column_offset].T, preferred_ele...]
    ppermute x2 -> x0, waiting for transfers between devices: 38.6 us -> none  [the longest x1 34 us: with_halo(): lax.ppermute(tail, axis, [(i, (i + 1) % count) for i in range(ends)])]
    another operation x9 -> x2, other arithmetic: 26.2 us -> 0.86 us  [on_device(): jnp.stack([jnp.concatenate([p0, -p1], axis=0), jnp.concatenate([p1, p0],...]
    all_to_all x2 -> x0, waiting for transfers between devices: 24.7 us -> none  [the longest x1 24.7 us: on_device(): lax.all_to_all(lon_modes, 'lat', split_axis=2, concat_axis=0, tiled=True)]
    unnamed x81 -> x12, local copies, waits for them, and re-layouts: 25.3 us -> 1.24 us
  transfers between devices with their start and end apart: 6 -> 0, of which waited for: 5 -> 0; matrix products, arithmetic and copies ran while one was open for 10% -> 0% of each run, Pallas kernels for 0% -> 0%
where the time goes in v1:
time: 216 us; the launch traced here: 214 us
  Pallas kernels  203 us (94%)
  local copies, waits for them, and re-layouts  8.91 us (4%)
    pallas_call x1, Pallas kernels, back(): pl.pallas_call(back_kernel, out_shape=[jax.ShapeDtypeStruct(a.shape, a.dt...  69.9 us
    pallas_call x3, Pallas kernels, call(): pl.pallas_call(kernel, out_shape=[jax.ShapeDtypeStruct(s, t) for s, t in...  47.1 us
    pallas_call x1, Pallas kernels, swap(): pl.pallas_call(swap_kernel, out_shape=jax.ShapeDtypeStruct(a.shape, a.dty...  44.4 us
    pallas_call x1, Pallas kernels, gather(): pl.pallas_call(gather_kernel, out_shape=jax.ShapeDtypeStruct((ROWS, 3, CO...  41.3 us

profile of v1, /device:TPU:8, one launch (start us, length us, event | category | flops | bytes accessed | tf_op | source)
XLA Modules:
  0.0 214.2 jit_solution(10409555825318954276)
XLA Ops:
  0.6 1.9 pad.12.g_ref
  2.5 0.0 copy-start.1
  2.5 41.3 %gather_rows.1.g_ref = bf16[4,3,256,1024]{3,2,1,0:T(8,128)(2,1)} custom-call(bf16[4,64,1024]{2,1,0:T(8,128)(2,1)} %pad.12.g_ref), custom_call_target="tpu_custom_call" | custom-call | tf_op jit(solution)/shard_map/gather_rows/pallas_call | solution.py:169
  43.9 0.0 copy-done.1
  43.9 0.8 copy.22
  44.6 1.1 copy.28
  45.7 22.4 %conv_terms.1 = (f32[768,1024]{1,0:T(8,128)}, bf16[1024,768]{1,0:T(8,128)(2,1)}, bf16[8,432,128]{2,1,0:T(8,128)(2,1)}) custom-call(bf16[4,3,256,1024]{3,2,1,0:T(8,128)(2,1)} %gather_rows.1.g_ref, bf16[4,192,900]{2,1,0:T(8,128)(2,1)} %bitcast.61, bf16[576,768]{1,0:T(8,128)(2,1)} %bitcast.57, bf16[1024,1024]{1,0:T(8,128)(2,1)} %constant.14.clone.ana_ref), custom_call_target="tpu_custom_call" | custom-call | flops 8000000000 | bytes 8388608 | tf_op jit(solution)/shard_map/conv_terms/pallas_call | solution.py:236
  68.2 0.0 copy-start
  68.2 44.4 %swap_modes.1 = bf16[64,16,768]{2,1,0:T(8,128)(2,1)} custom-call(bf16[64,16,768]{2,1,0:T(8,128)(2,1)} %bitcast.51), custom_call_target="tpu_custom_call" | custom-call | tf_op jit(solution)/shard_map/swap_modes/pallas_call | solution.py:311
  112.6 0.0 copy-done
  112.6 0.1 copy.23
  112.7 0.0 copy-start.2
  112.7 0.0 copy-start.3
  112.7 1.7 copy.25.u_ref
  114.4 0.0 copy-done.2
  114.4 0.1 concatenate.52
  114.5 0.0 copy-start.4
  114.5 0.1 concatenate.55
  114.7 0.8 maximum_maximum_fusion.m1_ref
  115.5 0.0 copy-done.3
  115.5 0.1 concatenate.63
  115.6 0.1 concatenate.61
  115.8 0.8 pad_maximum_fusion.m2_ref
  116.6 0.0 copy-done.4
  116.6 0.6 reshape.67.b1_ref
  117.3 17.8 %spectral_filter.1 = (bf16[1024,768]{1,0:T(8,128)(2,1)}, bf16[8,112,128]{2,1,0:T(8,128)(2,1)}) custom-call(bf16[1024,768]{1,0:T(8,128)(2,1)} %bitcast.50, bf16[7,256,384]{2,1,0:T(8,128)(2,1)} %copy.25.u_ref, bf16[7,128,1024]{2,1,0:T(8,128)(2,1)} %constant.15.clone.fwd_ref, bf16[1024,896]{1,0:T(8,128)(2,1)} %constant.16.clone.inv_ref, ...), custom_call_target="tpu_custom_call" | custom-call | flops 6000000000 | bytes 8388608 | tf_op jit(solution)/shard_map/spectral_filter/pallas_call | solution.py:236
  135.1 69.9 %swap_back.1 = (bf16[64,16,768]{2,1,0:T(8,128)(2,1)}, bf16[8,544,128]{2,1,0:T(8,128)(2,1)}) custom-call(bf16[64,16,768]{2,1,0:T(8,128)(2,1)} %bitcast.52, bf16[8,432,128]{2,1,0:T(8,128)(2,1)} %get-tuple-element.17.qc_ref, bf16[8,112,128]{2,1,0:T(8,128)(2,1)} %get-tuple-element.18.qf_ref), custom_call_target="tpu_custom_call" | custom-call | tf_op jit(solution)/shard_map/swap_back/pallas_call | solution.py:501
  205.0 6.8 %synthesis.1 = (bf16[768,900]{1,0:T(8,128)(2,1)}, f32[3,3,192,256]{3,2,1,0:T(8,128)}) custom-call(bf16[1024,768]{1,0:T(8,128)(2,1)} %bitcast.53, bf16[1024,1024]{1,0:T(8,128)(2,1)} %constant.18.clone.syn_ref, f32[768,1024]{1,0:T(8,128)} %get-tuple-element.20.cg_ref, bf16[8,544,128]{2,1,0:T(8,128)(2,1)} %get-tuple-element.21.q_ref), custom_call_target="tpu_custom_call" | custom-call | flops 1600000000 | bytes 8388608 | tf_op jit(solution)/shard_map/synthesis/pallas_call | solution.py:236
  211.8 1.0 slice.55
  212.8 0.8 slice_bitcast_fusion
  213.6 0.6 fusion
  (12 shorter events, 0.2 us)
Async XLA Ops:
  2.5 41.3 %copy-start.1 = (bf16[3,3,192,256]{3,2,1,0:T(8,128)(2,1)S(1)}, bf16[3,3,192,256]{3,2,1,0:T(8,128)(2,1)}, u32[]{:S(2)}) copy-start(bf16[3,3,192,256]{3,2,1,0:T(8,128)(2,1)} %param.14) | copy-start | bytes 2654212
  68.2 44.4 %copy-start = (bf16[7,256,2,2,96]{1,4,3,2,0:T(8,128)(2,1)S(1)}, bf16[7,256,2,2,96]{1,4,3,2,0:T(8,128)(2,1)}, u32[]{:S(2)}) copy-start(bf16[7,256,2,2,96]{1,4,3,2,0:T(8,128)(2,1)} %param.15) | copy-start | bytes 4128772
  112.7 1.7 copy-start.2
  112.7 2.8 %copy-start.3 = (bf16[2,2,96,96]{3,2,1,0:T(8,128)(2,1)S(1)}, bf16[2,2,96,96]{3,2,1,0:T(8,128)(2,1)}, u32[]{:S(2)}) copy-start(bf16[2,2,96,96]{3,2,1,0:T(8,128)(2,1)} %param.18) | copy-start | bytes 221188
  114.5 2.1 copy-start.4

commit v2 on v0

v2 whole, which is shorter than its diff:
```python
import functools
import math

import jax
import jax.numpy as jnp
import ml_dtypes
import numpy as np
from jax import lax
from jax.experimental import pallas as pl
from jax.experimental.pallas import tpu as pltpu
from jax.sharding import PartitionSpec as P

MESH = pl.DeviceIdType.MESH
F32, BF16 = jnp.float32, jnp.bfloat16
STEP = 4
LON, PAD = 900, 1024
NLAT = 64
ROWS = 4
NK = 7
KX = 448
CI, CO = 192, 256
BS = 96
PS = ROWS * BS
VMEM = 56 * 1024 * 1024
NT = (((1,), (1,)), ((), ()))
TN = (((0,), (0,)), ((), ()))
NN = (((1,), (0,)), ((), ()))


def dot(a, b, dims=NN):
    return lax.dot_general(a, b, dims, preferred_element_type=F32)


def lon_tables():
    q = np.arange(LON)[None, :]
    d, i, kk = np.meshgrid(np.arange(NLAT), np.arange(2), np.arange(8), indexing="ij")
    k = (d * NK + kk).reshape(-1, 1)
    i = i.reshape(-1, 1)
    live = (kk.reshape(-1, 1) < NK).astype(np.float64)
    angle = (k * q % LON) * (2.0 * math.pi / LON)
    base = np.where(i == 0, np.cos(angle), -np.sin(angle)) / math.sqrt(LON) * live
    weight = np.where(k == 0, 1.0, 2.0)
    pad = ((0, 0), (0, PAD - LON))
    ana = np.pad(base * weight, pad).astype(ml_dtypes.bfloat16)
    syn = np.pad(base, pad).astype(ml_dtypes.bfloat16)
    return ana, syn


def lat_tables():
    y = np.arange(NLAT)[:, None]
    l = np.arange(NLAT)[None, :]
    angle = (y * l % NLAT) * (2.0 * math.pi / NLAT)
    c, s = np.cos(angle) / 16.0, np.sin(angle) / 16.0
    small = np.array([[c, s], [-s, c]])
    fwd = np.zeros((NK, 2, NLAT, NLAT, 2, 8))
    for k in range(NK):
        fwd[k, :, :, :, :, k] = small.transpose(0, 2, 3, 1)
    fwd = fwd.reshape(NK, 2 * NLAT, 16 * NLAT)
    back = np.array([[c, -s], [s, c]])
    inv = np.zeros((NLAT, 2, 8, NK, 2, NLAT))
    for k in range(NK):
        inv[:, :, k, k] = back.transpose(3, 0, 1, 2)
    inv = inv.reshape(16 * NLAT, NK * 2 * NLAT)
    tw = np.zeros((2, ROWS, NLAT, 1))
    for p in range(ROWS):
        a = np.arange(NLAT) * p * (2.0 * math.pi / 256)
        tw[0, p, :, 0], tw[1, p, :, 0] = np.cos(a), np.sin(a)
    tw = np.repeat(tw[..., 0].transpose(0, 2, 1), BS, axis=2)
    return (
        fwd.astype(ml_dtypes.bfloat16),
        inv.astype(ml_dtypes.bfloat16),
        np.ascontiguousarray(tw).astype(np.float32),
    )


def shifted(x, s):
    if s == 0:
        return x
    lane = lax.broadcasted_iota(jnp.int32, x.shape, 1)
    if s > 0:
        return jnp.where(lane < s, pltpu.roll(x, PAD - LON + s, 1), pltpu.roll(x, s, 1))
    return jnp.where(lane >= LON + s, pltpu.roll(x, LON + s, 1), pltpu.roll(x, PAD + s, 1))


class Summing:
    def __init__(self, me, parts, in1, buf2, in2, buf4, out, send, recv):
        self.z, self.spot = me // 8, lax.rem(me, 8)
        self.parts, self.in1, self.buf2, self.in2 = parts, in1, buf2, in2
        self.buf4, self.out, self.send, self.recv = buf4, out, send, recv
        self.rows, self.slot = parts.shape[1], in2.shape[1]

    def copy(self, stage, o, at):
        z, spot = self.z, self.spot
        to_spot, to_z = lax.rem(spot + o, 8), lax.rem(z + o, 8)
        if stage == 0:
            src, dst, lat = self.parts.at[to_spot], self.in1.at[at], z * 8 + to_spot
        elif stage == 1:
            src, dst, lat = self.buf2.at[self.zrows(to_z), :], self.in2.at[at], to_z * 8 + spot
        elif stage == 2:
            src, dst = self.buf4.at[self.zrows(z), :], self.buf4.at[self.zrows(at), :]
            lat = to_z * 8 + spot
        else:
            src, dst, lat = self.buf4.at[pl.ds(0, self.rows), :], self.out.at[at], z * 8 + to_spot
        return pltpu.make_async_remote_copy(
            src_ref=src,
            dst_ref=dst,
            send_sem=self.send.at[stage, o],
            recv_sem=self.recv.at[stage, o],
            device_id={"lat": lat},
            device_id_type=MESH,
        )

    def zrows(self, i):
        return pl.ds(pl.multiple_of(i * self.slot, 16), self.slot)

    def start(self, stage):
        at = self.spot if stage in (0, 3) else self.z

        def go(o, carry):
            self.copy(stage, o, at).start()
            return carry

        lax.fori_loop(1, 8, go, 0)
        if stage == 0:
            self.in1[at] = self.parts[at]
        elif stage == 1:
            self.in2[at] = self.buf2[self.zrows(at), :]
        elif stage == 3:
            self.out[at] = self.buf4[0 : self.rows, :]

    def wait(self, stage):
        at = self.spot if stage in (0, 3) else self.z

        def done(o, carry):
            self.copy(stage, o, lax.rem(at - o + 8, 8)).wait()
            return carry

        lax.fori_loop(1, 8, done, 0)
        if stage == 0:
            total = self.in1[0].astype(F32)
            for i in range(1, 8):
                total = total + self.in1[i].astype(F32)
            self.buf2[0 : self.rows, :] = total.astype(BF16)
            rest = 8 * self.slot - self.rows
            self.buf2[self.rows :, :] = jnp.zeros((rest, 128), BF16)
        elif stage == 1:
            total = self.in2[0].astype(F32)
            for i in range(1, 8):
                total = total + self.in2[i].astype(F32)
            self.buf4[self.zrows(at), :] = total.astype(BF16)


class Swap:
    def __init__(self, me, a, r, send, recv):
        self.me, self.a, self.r, self.send, self.recv = me, a, r, send, recv

    def copy(self, n, to, source):
        return pltpu.make_async_remote_copy(
            src_ref=self.a.at[n, to],
            dst_ref=self.r.at[n, source],
            send_sem=self.send.at[n, to],
            recv_sem=self.recv.at[n, source],
            device_id={"lat": to},
            device_id_type=MESH,
        )

    def start(self, n, first, count):
        def go(i, carry):
            to = first + i

            @pl.when(to != self.me)
            def _():
                self.copy(n, to, self.me).start()

            return carry

        lax.fori_loop(0, count, go, 0)

    def wait_recv(self, n):
        self.r[n, self.me] = self.a[n, self.me]

        def done(o, carry):
            other = lax.rem(self.me + o, NLAT)
            self.copy(n, other, other).wait_recv()
            return carry

        lax.fori_loop(1, NLAT, done, 0)

    def wait_send(self, n):
        def done(o, carry):
            other = lax.rem(self.me + o, NLAT)
            self.copy(n, other, other).wait_send()
            return carry

        lax.fori_loop(1, NLAT, done, 0)


ROOT = math.sqrt(2.0 / math.pi)
QC, QCZ, QF, QFZ = 432, 64, 112, 16


def fused_kernel(
    og_ref, ci_hbm, cw_hbm, u_hbm, w1_ref, b1_ref, w2_ref, tw_ref, ana_hbm, syn_hbm, fwd_hbm, inv_hbm,
    out_ref, sumc_ref, sumf_ref,
    g_ref, ci_ref, w_ref, u_ref, ana_ref, syn_ref, fwd_ref, inv_ref, m1_ref, m2_ref,
    cg_ref, hg_ref, acc_ref, cib_ref, a_ref, r_ref, b_ref, r2_ref, z_ref, e_ref,
    g1_ref, g2_ref, bias_ref, part_ref,
    qc_ref, qf_ref, c1_ref, c2_ref, c3_ref, c4_ref, f1_ref, f2_ref, f3_ref, f4_ref,
    loads, wloads, gsend, grecv, asend, arecv, bsend, brecv, csend, crecv, fsend, frecv,
):
    me = lax.axis_index("lat")
    ch = lax.axis_index("ch")
    zed = me // 8
    xlo = lax.rem(me, 2)
    near = 2 * xlo
    far = 2 - near
    pair = me + 1 - 2 * xlo
    ch2 = lax.rem(ch + 2, 4)
    core = ch + 1 - 2 * lax.rem(ch, 2)
    core2 = lax.rem(core + 2, 4)
    nxt = lax.rem(me + 2 - 4 * xlo + NLAT, NLAT)

    barrier = pltpu.get_barrier_semaphore()

    def hello(o, carry):
        dev = (lax.rem(me + o, NLAT), ch)
        pl.semaphore_signal(barrier, inc=1, device_id=dev, device_id_type=MESH)
        return carry

    for dev in ((me, core), (pair, ch2)):
        pl.semaphore_signal(barrier, inc=1, device_id=dev, device_id_type=MESH)
    lax.fori_loop(1, NLAT, hello, 0)

    def load(i):
        pairs = (
            (ci_hbm, ci_ref), (u_hbm, u_ref), (ana_hbm, ana_ref),
            (fwd_hbm, fwd_ref), (inv_hbm, inv_ref), (syn_hbm, syn_ref),
        )
        return pltpu.make_async_copy(pairs[i][0], pairs[i][1], loads.at[i])

    wcopies = []
    for a in range(3):
        for b in range(3):
            wcopies.append(
                pltpu.make_async_copy(
                    cw_hbm.at[a, b],
                    w_ref.at[pl.ds(b * CI, CI), pl.ds(a * CO, CO)],
                    wloads.at[a * 3 + b],
                )
            )
    for copy in wcopies:
        copy.start()
    for i in range(6):
        load(i).start()

    def rows(c):
        return pl.ds(pl.multiple_of(c * 64, 64), 64)

    def at(p, slot, c):
        return g_ref.at[p, slot, rows(c), :]

    blank = jnp.zeros((64, PAD - LON), F32)
    for p in range(ROWS):
        g_ref[p, 1, rows(ch), :] = jnp.concatenate(
            [og_ref[p].astype(F32), blank], axis=1
        ).astype(BF16)
    pl.semaphore_wait(barrier, NLAT + 1)

    started = []

    def hop(src, dst, kind, p, dev):
        return pltpu.make_async_remote_copy(
            src_ref=src,
            dst_ref=dst,
            send_sem=gsend.at[kind, p],
            recv_sem=grecv.at[kind, p],
            device_id=dev,
            device_id_type=MESH,
        )

    def go(src, dst, kind, p, dev):
        copy = hop(src, dst, kind, p, dev)
        copy.start()

    def got(kind, p, dst):
        hop(dst, dst, kind, p, (me, core)).wait_recv()

    for p in range(ROWS):
        go(at(p, 1, ch), at(p, far, ch), 0, p, (pair, ch))
        go(at(p, 1, ch), at(p, far, ch), 1, p, (pair, ch2))
    for p in range(ROWS):
        go(at(p, 1, ch), at(p, 1, ch), 5, p, (me, core))

    for w, m_ref in ((w1_ref, m1_ref), (w2_ref, m2_ref)):
        for n in range(2):
            re, im = w[n, 0], w[n, 1]
            m_ref[n, 0:BS, :] = jnp.concatenate([re, im], axis=1)
            m_ref[n, BS:, :] = jnp.concatenate([-im, re], axis=1)
    for copy in wcopies:
        copy.wait()

    @pl.when(me == 0)
    def _():
        w_ref[:, 2 * CO :] = jnp.zeros((3 * CI, CO), BF16)

    @pl.when(me == NLAT - 1)
    def _():
        w_ref[:, :CO] = jnp.zeros((3 * CI, CO), BF16)

    for p in range(ROWS):
        got(0, p, at(p, near, ch))
        go(at(p, near, ch), at(p, far, ch), 3, p, (nxt, ch))
        if p < 2:
            go(at(p, near, ch), at(p, 1, ch), 2, p, (pair, ch2))
        got(1, p, at(p, near, ch2))
        go(at(p, near, ch2), at(p, far, ch2), 4, p, (nxt, ch))
        if p >= 2:
            go(at(p, near, ch2), at(p, 1, ch2), 2, p, (pair, ch))
        go(at(p, near, ch), at(p, near, ch), 6, p, (me, core))
        go(at(p, near, ch2), at(p, near, ch2), 7, p, (me, core))

    def conv_row(p, carry):
        got(2, p, at(p, 1, ch2))
        go(at(p, 1, ch2), at(p, 1, ch2), 8, p, (me, core))
        got(3, p, at(p, far, ch))
        go(at(p, far, ch), at(p, far, ch), 9, p, (me, core))
        got(4, p, at(p, far, ch2))
        go(at(p, far, ch2), at(p, far, ch2), 10, p, (me, core))
        got(5, p, at(p, 1, core))
        got(6, p, at(p, near, core))
        got(7, p, at(p, near, core2))
        got(8, p, at(p, 1, core2))
        got(9, p, at(p, far, core))
        got(10, p, at(p, far, core2))
        g = g_ref[p].reshape(3 * CO, PAD)
        for b in range(3):
            part_ref[b] = dot(w_ref[b * CI : (b + 1) * CI, :], g)
        total = part_ref[1]
        for b in (0, 2):
            total = total + shifted(part_ref[b], STEP * (b - 1))
        where = pl.ds(pl.multiple_of(p * BS, 16), BS)
        for n in range(2):
            cg_ref[n, where, :] = total[n * BS : (n + 1) * BS]
            hg_ref[n, where, :] = total[n * BS : (n + 1) * BS].astype(BF16)
        return carry

    lax.fori_loop(0, ROWS, conv_row, 0)

    there = Swap(me, a_ref, r_ref, asend, arecv)
    load(2).wait()

    def analyse(t, carry):
        n = t // 4
        c = lax.rem(zed // 2 + 2 + t, 4)
        where = pl.ds(pl.multiple_of(c * 256, 256), 256)
        block = dot(ana_ref[where, :], hg_ref[n], NT).astype(BF16)
        a_ref[n, pl.ds(c * 16, 16)] = block.reshape(16, 16, PS)
        there.start(n, c * 16, 16)
        return carry

    lax.fori_loop(0, 8, analyse, 0)

    load(0).wait()
    acc_ref[...] = jnp.zeros_like(acc_ref)
    blank2 = jnp.zeros((CI, PAD - LON), F32)

    def kernel_row(p, carry):
        g = g_ref[p].reshape(3 * CO, PAD)
        x = jnp.concatenate([ci_ref[p].astype(F32), blank2], axis=1)
        for b in range(3):
            cib_ref[b * CI : (b + 1) * CI, :] = shifted(x, -STEP * (b - 1)).astype(BF16)
        for b in range(3):
            acc_ref[b * CI : (b + 1) * CI, :] += dot(cib_ref[b * CI : (b + 1) * CI, :], g, NT)
        return carry

    lax.fori_loop(0, ROWS, kernel_row, 0)

    @pl.when(me == 0)
    def _():
        acc_ref[:, 2 * CO :] = jnp.zeros((3 * CI, CO), F32)

    @pl.when(me == NLAT - 1)
    def _():
        acc_ref[:, :CO] = jnp.zeros((3 * CI, CO), F32)

    for rr in range(4):
        for cc in range(2):
            for t in range(3):
                col = cc * 384 + t * 128
                qc_ref[rr * 2 + cc, t * 144 : (t + 1) * 144, :] = acc_ref[
                    rr * 144 : (rr + 1) * 144, col : col + 128
                ].astype(BF16)
    sumc = Summing(me, qc_ref, c1_ref, c2_ref, c3_ref, c4_ref, sumc_ref, csend, crecv)
    sumf = Summing(me, qf_ref, f1_ref, f2_ref, f3_ref, f4_ref, sumf_ref, fsend, frecv)
    sumc.start(0)

    home = Swap(me, b_ref, r2_ref, bsend, brecv)
    load(1).wait()
    load(3).wait()
    load(4).wait()
    qf_ref[...] = jnp.zeros_like(qf_ref)

    def block_filter(n, carry):
        there.wait_recv(n)
        g1_ref[...] = jnp.zeros_like(g1_ref)
        g2_ref[...] = jnp.zeros_like(g2_ref)
        bias_ref[...] = jnp.zeros_like(bias_ref)
        for half in range(2):
            at_k = slice(half * 448, (half + 1) * 448)
            z_ref[at_k, :] = dot(fwd_ref[at_k, :], r_ref[n].reshape(16 * NLAT, PS))
        b1 = b1_ref[n].astype(F32)
        b1 = jnp.concatenate([b1[0:1], b1[1:2]], axis=1)

        def mode(k, carry2):
            top = pl.multiple_of(k * 2 * NLAT, 2 * NLAT)
            zr, zi = z_ref[pl.ds(top, NLAT), :], z_ref[pl.ds(top + NLAT, NLAT), :]
            c, s = tw_ref[0], tw_ref[1]
            zr, zi = zr * c + zi * s, zi * c - zr * s
            wr = [zr[:, p * BS : (p + 1) * BS] for p in range(ROWS)]
            wi = [zi[:, p * BS : (p + 1) * BS] for p in range(ROWS)]
            ar, ai = wr[0] + wr[2], wi[0] + wi[2]
            br, bi = wr[0] - wr[2], wi[0] - wi[2]
            cr, ci = wr[1] + wr[3], wi[1] + wi[3]
            dr, di = wr[1] - wr[3], wi[1] - wi[3]
            vr = jnp.concatenate([ar + cr, br + di, ar - cr, br - di], axis=0)
            vi = jnp.concatenate([ai + ci, bi - dr, ai - ci, bi + dr], axis=0)
            v = jnp.concatenate([vr, vi], axis=1).astype(BF16)

            u = u_ref[k, n]
            pre = dot(u, m1_ref[n], TN) + b1
            sq = pre * pre
            th = jnp.tanh(ROOT * pre * (1.0 + 0.044715 * sq))
            act = (0.5 * pre * (1.0 + th)).astype(BF16)
            slope = 0.5 * (1.0 + th) + 0.5 * pre * (1.0 - th * th) * (
                ROOT * (1.0 + 3.0 * 0.044715 * sq)
            )
            d_pre = (dot(v, m2_ref[n], NT) * slope).astype(BF16)
            g2_ref[...] += dot(act, v, TN)
            g1_ref[...] += dot(u, d_pre)
            bias_ref[0:1, :] += jnp.sum(d_pre.astype(F32), axis=0, keepdims=True)
            bias_ref[1:2, :] += jnp.sum(v.astype(F32), axis=0, keepdims=True)
            x = dot(d_pre, m1_ref[n], NT).astype(BF16).astype(F32)
            xr = [x[j * NLAT : (j + 1) * NLAT, :BS] for j in range(4)]
            xi = [x[j * NLAT : (j + 1) * NLAT, BS:] for j in range(4)]
            ar, ai = xr[0] + xr[2], xi[0] + xi[2]
            br, bi = xr[0] - xr[2], xi[0] - xi[2]
            cr, ci = xr[1] + xr[3], xi[1] + xi[3]
            dr, di = xr[1] - xr[3], xi[1] - xi[3]
            er = jnp.concatenate([ar + cr, br - di, ar - cr, br + di], axis=1)
            ei = jnp.concatenate([ai + ci, bi + dr, ai - ci, bi - dr], axis=1)
            e_ref[pl.ds(top, NLAT), :] = (er * c - ei * s).astype(BF16)
            e_ref[pl.ds(top + NLAT, NLAT), :] = (ei * c + er * s).astype(BF16)
            return carry2

        lax.fori_loop(0, NK, mode, 0)
        for w, (grad, row) in enumerate(((g1_ref, 0), (g2_ref, 1))):
            full = grad[...]
            halves = (full[:BS, :BS] + full[BS:, BS:], full[:BS, BS:] - full[BS:, :BS])
            for part in range(2):
                j = w * 4 + n * 2 + part
                qf_ref[j, 0:BS, 0:BS] = halves[part].astype(BF16)
                tail = bias_ref[row : row + 1, part * BS : (part + 1) * BS]
                qf_ref[j, BS:QF, 0:BS] = jnp.broadcast_to(tail, (QF - BS, BS)).astype(BF16)

        @pl.when(n == 1)
        def _():
            sumf.start(0)

        def inverse(j, carry2):
            c = lax.rem(zed // 2 + 2 + j, 4)
            where = pl.ds(pl.multiple_of(c * 256, 256), 256)
            block = dot(inv_ref[where, :], e_ref[...]).astype(BF16)
            b_ref[n, pl.ds(c * 16, 16)] = block.reshape(16, 16, PS)
            home.start(n, c * 16, 16)
            return carry2

        lax.fori_loop(0, 4, inverse, 0)

        @pl.when(n == 0)
        def _():
            sumc.wait(0)
            sumc.start(1)

        return carry

    lax.fori_loop(0, 2, block_filter, 0)
    sumc.wait(1)
    sumc.start(2)
    sumf.wait(0)
    sumf.start(1)
    sumc.wait(2)
    sumc.start(3)
    load(5).wait()

    def synthesis(n):
        home.wait_recv(n)
        for m in range(3):
            lanes = slice(m * 128, (m + 1) * 128)
            modes = r2_ref[n].reshape(16 * NLAT, PS)[:, lanes]
            part = (dot(modes, syn_ref[...], TN) + cg_ref[n, lanes, :])[:, :LON].astype(BF16)
            r = 0
            while r < 128:
                p, s = divmod(m * 128 + r, BS)
                size = min(BS - s, 128 - r)
                out_ref[p, n * BS + s : n * BS + s + size, :] = part[r : r + size]
                r += size

    synthesis(0)
    sumf.wait(1)
    sumf.start(2)
    sumf.wait(2)
    sumf.start(3)
    synthesis(1)
    sumc.wait(3)
    sumf.wait(3)
    for n in range(2):
        there.wait_send(n)
        home.wait_send(n)

    def gather_sent(p, carry):
        for kind in range(11):
            hop(at(p, 1, ch), at(p, 1, ch), kind, p, (me, core)).wait_send()
        return carry

    lax.fori_loop(0, ROWS, gather_sent, 0)


def fused(*args):
    vmem, anywhere = pl.BlockSpec(memory_space=pltpu.VMEM), pl.BlockSpec(memory_space=pl.ANY)
    dma = pltpu.SemaphoreType.DMA
    half, wide = BF16, F32
    scratch = [
        ((ROWS, 3, CO, PAD), half), ((ROWS, CI, LON), half), ((3 * CI, 3 * CO), half),
        ((NK, 2, CI, 256), half), ((16 * NLAT, PAD), half), ((16 * NLAT, PAD), half),
        ((NK * 2 * NLAT, 16 * NLAT), half), ((16 * NLAT, NK * 2 * NLAT), half),
        ((2, CI, CI), half), ((2, CI, CI), half),
        ((2, PS, PAD), wide), ((2, PS, PAD), half), ((3 * CI, 3 * CO), wide), ((3 * CI, PAD), half),
        ((2, NLAT, 16, PS), half), ((2, NLAT, 16, PS), half), ((2, NLAT, 16, PS), half),
        ((2, NLAT, 16, PS), half), ((NK * 2 * NLAT, PS), wide), ((NK * 2 * NLAT, PS), half),
        ((CI, CI), wide), ((CI, CI), wide), ((8, CI), wide), ((3, CI, PAD), wide),
        ((8, QC, 128), half), ((8, QF, 128), half),
        ((8, QC, 128), half), ((8 * QCZ, 128), half), ((8, QCZ, 128), half), ((8 * QCZ, 128), half),
        ((8, QF, 128), half), ((8 * QFZ, 128), half), ((8, QFZ, 128), half), ((8 * QFZ, 128), half),
    ]
    return pl.pallas_call(
        fused_kernel,
        out_shape=[
            jax.ShapeDtypeStruct((ROWS, CI, LON), BF16),
            jax.ShapeDtypeStruct((8, QC, 128), BF16),
            jax.ShapeDtypeStruct((8, QF, 128), BF16),
        ],
        in_specs=[vmem] + [anywhere] * 3 + [vmem] * 4 + [anywhere] * 4,
        out_specs=[vmem] * 3,
        scratch_shapes=[pltpu.VMEM(s, t) for s, t in scratch]
        + [
            dma((6,)), dma((9,)), dma((11, ROWS)), dma((11, ROWS)),
            dma((2, NLAT)), dma((2, NLAT)), dma((2, NLAT)), dma((2, NLAT)),
            dma((4, 8)), dma((4, 8)), dma((4, 8)), dma((4, 8)),
        ],
        compiler_params=pltpu.CompilerParams(
            collective_id=0, has_side_effects=True, vmem_limit_bytes=VMEM
        ),
        cost_estimate=pl.CostEstimate(flops=16_000_000_000, bytes_accessed=32 << 20, transcendentals=0),
        name="block_backward",
    )(*args)


def unpack_kernel(c_ref, f_ref, gc_ref, w1_ref, b1_ref, w2_ref, b2_ref):
    for rr in range(4):
        for cc in range(2):
            for t in range(3):
                a, o = divmod(cc * 384 + t * 128, CO)
                r = rr * 144
                while r < (rr + 1) * 144:
                    b, c = divmod(r, CI)
                    n = min(CI - c, (rr + 1) * 144 - r)
                    at = t * 144 + r - rr * 144
                    gc_ref[a, b, c : c + n, o : o + 128] = c_ref[rr * 2 + cc, at : at + n, :].astype(F32)
                    r += n
    for w, (w_ref, b_ref) in enumerate(((w1_ref, b1_ref), (w2_ref, b2_ref))):
        for n in range(2):
            for part in range(2):
                block = f_ref[w * 4 + n * 2 + part].astype(F32)
                w_ref[n, part] = block[:BS, :BS]
                b_ref[n, part : part + 1, :] = block[BS : BS + 1, :BS]


def unpack(sumc, sumf):
    vmem = pl.BlockSpec(memory_space=pltpu.VMEM)
    outs = [(3, 3, CI, CO), (2, 2, BS, BS), (2, 2, BS), (2, 2, BS, BS), (2, 2, BS)]
    return pl.pallas_call(
        unpack_kernel,
        out_shape=[jax.ShapeDtypeStruct(s, F32) for s in outs],
        in_specs=[vmem] * 2,
        out_specs=[vmem] * 5,
        compiler_params=pltpu.CompilerParams(vmem_limit_bytes=VMEM),
        name="lay_out",
    )(sumc, sumf)


def on_device(output_gradient, conv_in, conv_weight, modes, w1, b1, w2):
    ana, syn = lon_tables()
    fwd, inv, tw = lat_tables()
    fwd = fwd.reshape(NK * 2 * NLAT, 16 * NLAT)
    grad_in, sumc, sumf = fused(
        jnp.transpose(output_gradient, (0, 2, 1)),
        jnp.transpose(conv_in, (0, 2, 1)),
        conv_weight,
        jnp.transpose(modes, (0, 2, 3, 4, 1)).reshape(NK, 2, CI, 256),
        w1, b1, w2, tw, ana, syn, fwd, inv,
    )
    grad_in = jnp.transpose(grad_in, (0, 2, 1))
    return (grad_in, *unpack(sumc, sumf))


def solution(mesh):
    placed = (
        P("lat", None, "ch"),
        P("lat", None, "ch"),
        P(None, None, "ch", None),
        P("lat", None, "ch", None, None),
        P("ch", None, None, None),
        P("ch", None, None),
        P("ch", None, None, None),
    )
    return jax.shard_map(
        on_device,
        mesh=mesh,
        in_specs=placed,
        out_specs=(
            P("lat", None, "ch"),
            P(None, None, "ch", None),
            P("ch", None, None, None),
            P("ch", None, None),
            P("ch", None, None, None),
            P("ch", None, None),
        ),
        check_vma=False,
    )
```

time: 888 us -> 151 us (0.17)
  waiting for transfers between devices: 503 us -> 0 us
  blocking collectives: 172 us -> 0 us
  Pallas kernels: 0 us -> 146 us
  local copies, waits for them, and re-layouts: 70.7 us -> 2.67 us
  matrix products: 63.9 us -> 0 us
  starting transfers between devices: 28.1 us -> 0 us
  other arithmetic: 26.9 us -> 0 us
  between operations: 14.8 us -> 0.64 us
    psum x1 -> x0, waiting for transfers between devices: 421 us -> none  [on_device(): grad_conv = lax.psum(kernel_local, 'lat')]
    psum x1 -> x0, blocking collectives: 172 us -> none  [on_device(): lax.psum((first_local, first_bias, second_local, second_bias), 'lat')]
    pallas_call x0 -> x2, Pallas kernels: none -> 146 us  [the longest x1 144 us: fused(): pl.pallas_call(fused_kernel, out_shape=[jax.ShapeDtypeStruct((ROWS, CI, L...]
    dot_general x27 -> x0, matrix products: 63.9 us -> none  [the longest x9 19.8 us: on_device(): jnp.dot(flat_tap, conv_weight[row_offset, column_offset].T, preferred_ele...]
    ppermute x2 -> x0, waiting for transfers between devices: 38.6 us -> none  [the longest x1 34 us: with_halo(): lax.ppermute(tail, axis, [(i, (i + 1) % count) for i in range(ends)])]
    another operation x9 -> x0, other arithmetic: 26.2 us -> none
    all_to_all x2 -> x0, waiting for transfers between devices: 24.7 us -> none  [the longest x1 24.7 us: on_device(): lax.all_to_all(lon_modes, 'lat', split_axis=2, concat_axis=0, tiled=True)]
    unnamed x81 -> x1, local copies, waits for them, and re-layouts: 25.3 us -> 2.67 us
  transfers between devices with their start and end apart: 6 -> 0, of which waited for: 5 -> 0; matrix products, arithmetic and copies ran while one was open for 10% -> 0% of each run, Pallas kernels for 0% -> 0%
where the time goes in v2:
time: 151 us; the launch traced here: 149 us
  Pallas kernels  146 us (97%)
  local copies, waits for them, and re-layouts  2.67 us (2%)
    pallas_call x1, Pallas kernels, fused(): pl.pallas_call(fused_kernel, out_shape=[jax.ShapeDtypeStruct((ROWS, CI, L...  144 us

profile of v2, /device:TPU:8, one launch (start us, length us, event | category | flops | bytes accessed | tf_op | source)
XLA Modules:
  0.0 149.4 jit_solution(741264065739452723)
XLA Ops:
  0.6 143.5 %block_backward.1 = (bf16[4,192,900]{2,1,0:T(8,128)(2,1)}, bf16[8,432,128]{2,1,0:T(8,128)(2,1)}, bf16[8,112,128]{2,1,0:T(8,128)(2,1)}) custom-call(bf16[4,64,900]{2,1,0:T(8,128)(2,1)} %bitcast.9, bf16[4,192,900]{2,1,0:T(8,128)(2,1)} %bitcast.7, bf16[3,3,192,256]{3,2,1,0:T(8,128)(2,1)} %cw_hbm.1, bf16[7,2,192,256]{3,2,1,0:T(8,128)(2,1)} %bitcast.8, ...), custom_call_target="tpu_custom_call" | custom-call | flops 16000000000 | bytes 33554432 | tf_op jit(solution)/shard_map/block_backward/pallas_call | solution.py:545
  144.2 2.6 %lay_out.1 = (f32[3,3,192,256]{3,2,1,0:T(8,128)}, f32[2,2,96,96]{3,2,1,0:T(8,128)}, f32[2,2,96]{2,1,0:T(2,128)}, f32[2,2,96,96]{3,2,1,0:T(8,128)}, f32[2,2,96]{2,1,0:T(2,128)}) custom-call(bf16[8,432,128]{2,1,0:T(8,128)(2,1)} %get-tuple-element.15.c_ref, bf16[8,112,128]{2,1,0:T(8,128)(2,1)} %get-tuple-element.16.f_ref), custom_call_target="tpu_custom_call" | custom-call | tf_op jit(solution)/shard_map/lay_out/pallas_call | solution.py:591
  146.7 2.7 %copy.19 = bf16[4,900,192]{1,2,0:T(8,128)(2,1)} copy(bf16[4,900,192]{1,2,0:T(8,128)(2,1)} %bitcast.6) | data formatting | bytes 2764800

commit v3 on v2

--- a/solution.py
+++ b/solution.py
@@ -164,9 +164,9 @@
             device_id_type=MESH,
         )
 
-    def start(self, n, first, count):
+    def start(self, n, z):
         def go(i, carry):
-            to = first + i
+            to = z * 8 + i
 
             @pl.when(to != self.me)
             def _():
@@ -174,7 +174,7 @@
 
             return carry
 
-        lax.fori_loop(0, count, go, 0)
+        lax.fori_loop(0, 8, go, 0)
 
     def wait_recv(self, n):
         self.r[n, self.me] = self.a[n, self.me]
@@ -197,6 +197,7 @@
 
 ROOT = math.sqrt(2.0 / math.pi)
 QC, QCZ, QF, QFZ = 432, 64, 112, 16
+LAST = ROWS - 1
 
 
 def fused_kernel(
@@ -204,9 +205,9 @@
     out_ref, sumc_ref, sumf_ref,
     g_ref, ci_ref, w_ref, u_ref, ana_ref, syn_ref, fwd_ref, inv_ref, m1_ref, m2_ref,
     cg_ref, hg_ref, acc_ref, cib_ref, a_ref, r_ref, b_ref, r2_ref, z_ref, e_ref,
-    g1_ref, g2_ref, bias_ref, part_ref,
+    g1_ref, g2_ref, bias_ref, part_ref, relay_ref, act_ref, slope_ref, v_ref, d_ref, x_ref,
     qc_ref, qf_ref, c1_ref, c2_ref, c3_ref, c4_ref, f1_ref, f2_ref, f3_ref, f4_ref,
-    loads, wloads, gsend, grecv, asend, arecv, bsend, brecv, csend, crecv, fsend, frecv,
+    ready, loads, wloads, uloads, gsend, grecv, asend, arecv, bsend, brecv, csend, crecv, fsend, frecv,
 ):
     me = lax.axis_index("lat")
     ch = lax.axis_index("ch")
@@ -219,21 +220,24 @@
     core = ch + 1 - 2 * lax.rem(ch, 2)
     core2 = lax.rem(core + 2, 4)
     nxt = lax.rem(me + 2 - 4 * xlo + NLAT, NLAT)
+    prv = lax.rem(me - 2 + 4 * xlo + NLAT, NLAT)
 
     barrier = pltpu.get_barrier_semaphore()
 
+    spot = lax.rem(me, 8)
+    for dev in ((pair, ch), (pair, ch2), (me, core), (nxt, ch), (prv, ch)):
+        pl.semaphore_signal(barrier, inc=1, device_id=dev, device_id_type=MESH)
+
     def hello(o, carry):
-        dev = (lax.rem(me + o, NLAT), ch)
-        pl.semaphore_signal(barrier, inc=1, device_id=dev, device_id_type=MESH)
+        for lat in (zed * 8 + lax.rem(spot + o, 8), lax.rem(zed + o, 8) * 8 + spot):
+            pl.semaphore_signal(barrier, inc=1, device_id=(lat, ch), device_id_type=MESH)
         return carry
 
-    for dev in ((me, core), (pair, ch2)):
-        pl.semaphore_signal(barrier, inc=1, device_id=dev, device_id_type=MESH)
-    lax.fori_loop(1, NLAT, hello, 0)
+    lax.fori_loop(1, 8, hello, 0)
 
     def load(i):
         pairs = (
-            (ci_hbm, ci_ref), (u_hbm, u_ref), (ana_hbm, ana_ref),
+            (ci_hbm, ci_ref), (ana_hbm, ana_ref),
             (fwd_hbm, fwd_ref), (inv_hbm, inv_ref), (syn_hbm, syn_ref),
         )
         return pltpu.make_async_copy(pairs[i][0], pairs[i][1], loads.at[i])
@@ -250,7 +254,17 @@
             )
     for copy in wcopies:
         copy.start()
-    for i in range(6):
+    ucopies = []
+    for n in range(2):
+        for k in range(NK):
+            ucopies.append(
+                pltpu.make_async_copy(
+                    u_hbm.at[k, n], u_ref.at[n, :, pl.ds(k * 256, 256)], uloads.at[n * NK + k]
+                )
+            )
+    for copy in ucopies:
+        copy.start()
+    for i in range(5):
         load(i).start()
 
     def rows(c):
@@ -264,7 +278,13 @@
         g_ref[p, 1, rows(ch), :] = jnp.concatenate(
             [og_ref[p].astype(F32), blank], axis=1
         ).astype(BF16)
-    pl.semaphore_wait(barrier, NLAT + 1)
+    pl.semaphore_wait(barrier, 5 + 14)
+
+    def plane_here(o, carry):
+        lat = lax.rem(zed + o, 8) * 8 + spot
+        pl.semaphore_signal(ready, inc=1, device_id=(lat, ch), device_id_type=MESH)
+        return carry
+
 
     started = []
 
@@ -288,8 +308,12 @@
     for p in range(ROWS):
         go(at(p, 1, ch), at(p, far, ch), 0, p, (pair, ch))
         go(at(p, 1, ch), at(p, far, ch), 1, p, (pair, ch2))
+        if p == 0:
+            go(at(LAST, 1, ch), relay_ref, 11, LAST, (prv, ch))
     for p in range(ROWS):
         go(at(p, 1, ch), at(p, 1, ch), 5, p, (me, core))
+
+    lax.fori_loop(1, 8, plane_here, 0)
 
     for w, m_ref in ((w1_ref, m1_ref), (w2_ref, m2_ref)):
         for n in range(2):
@@ -309,13 +333,19 @@
 
     for p in range(ROWS):
         got(0, p, at(p, near, ch))
-        go(at(p, near, ch), at(p, far, ch), 3, p, (nxt, ch))
+        if p < LAST:
+            go(at(p, near, ch), at(p, far, ch), 3, p, (nxt, ch))
         if p < 2:
             go(at(p, near, ch), at(p, 1, ch), 2, p, (pair, ch2))
         got(1, p, at(p, near, ch2))
-        go(at(p, near, ch2), at(p, far, ch2), 4, p, (nxt, ch))
+        if p < LAST:
+            go(at(p, near, ch2), at(p, far, ch2), 4, p, (nxt, ch))
         if p >= 2:
             go(at(p, near, ch2), at(p, 1, ch2), 2, p, (pair, ch))
+        if p == 0:
+            got(11, LAST, relay_ref)
+            go(relay_ref, at(LAST, near, ch), 3, LAST, (pair, ch))
+            go(relay_ref, at(LAST, near, ch), 4, LAST, (pair, ch2))
         go(at(p, near, ch), at(p, near, ch), 6, p, (me, core))
         go(at(p, near, ch2), at(p, near, ch2), 7, p, (me, core))
 
@@ -347,15 +377,19 @@
     lax.fori_loop(0, ROWS, conv_row, 0)
 
     there = Swap(me, a_ref, r_ref, asend, arecv)
-    load(2).wait()
+    load(1).wait()
+    pl.semaphore_wait(ready, 7)
+
+    def plane(j):
+        half = (j + 1) // 2
+        return lax.rem(zed + 4 + half - 2 * half * lax.rem(j, 2), 8)
 
     def analyse(t, carry):
-        n = t // 4
-        c = lax.rem(zed // 2 + 2 + t, 4)
-        where = pl.ds(pl.multiple_of(c * 256, 256), 256)
+        n, z = t // 8, plane(lax.rem(t, 8))
+        where = pl.ds(pl.multiple_of(z * 128, 128), 128)
         block = dot(ana_ref[where, :], hg_ref[n], NT).astype(BF16)
-        a_ref[n, pl.ds(c * 16, 16)] = block.reshape(16, 16, PS)
-        there.start(n, c * 16, 16)
+        a_ref[n, pl.ds(z * 8, 8)] = block.reshape(8, 16, PS)
+        there.start(n, z)
         return carry
 
     lax.fori_loop(0, 8, analyse, 0)
@@ -393,25 +427,44 @@
     sumc = Summing(me, qc_ref, c1_ref, c2_ref, c3_ref, c4_ref, sumc_ref, csend, crecv)
     sumf = Summing(me, qf_ref, f1_ref, f2_ref, f3_ref, f4_ref, sumf_ref, fsend, frecv)
     sumc.start(0)
+    lax.fori_loop(8, 16, analyse, 0)
 
     home = Swap(me, b_ref, r2_ref, bsend, brecv)
-    load(1).wait()
+    load(2).wait()
     load(3).wait()
-    load(4).wait()
     qf_ref[...] = jnp.zeros_like(qf_ref)
 
+    for copy in ucopies:
+        copy.wait()
+
+    def saved(i, carry):
+        n, k = i // NK, lax.rem(i, NK)
+        here = pl.ds(pl.multiple_of(k * 256, 256), 256)
+        b1 = b1_ref[n].astype(F32)
+        b1 = jnp.concatenate([b1[0:1], b1[1:2]], axis=1)
+        pre = dot(u_ref[n, :, here], m1_ref[n], TN) + b1
+        sq = pre * pre
+        th = jnp.tanh(ROOT * pre * (1.0 + 0.044715 * sq))
+        act_ref[n, :, here] = jnp.transpose(0.5 * pre * (1.0 + th)).astype(BF16)
+        slope_ref[n, here, :] = 0.5 * (1.0 + th) + 0.5 * pre * (1.0 - th * th) * (
+            ROOT * (1.0 + 3.0 * 0.044715 * sq)
+        )
+        return carry
+
     def block_filter(n, carry):
+        lax.fori_loop(n * NK, n * NK + NK, saved, 0)
+
+        @pl.when(n == 0)
+        def _():
+            sumc.wait(0)
+            sumc.start(1)
+
         there.wait_recv(n)
-        g1_ref[...] = jnp.zeros_like(g1_ref)
-        g2_ref[...] = jnp.zeros_like(g2_ref)
-        bias_ref[...] = jnp.zeros_like(bias_ref)
         for half in range(2):
             at_k = slice(half * 448, (half + 1) * 448)
             z_ref[at_k, :] = dot(fwd_ref[at_k, :], r_ref[n].reshape(16 * NLAT, PS))
-        b1 = b1_ref[n].astype(F32)
-        b1 = jnp.concatenate([b1[0:1], b1[1:2]], axis=1)
-
-        def mode(k, carry2):
+
+        def radix(k, carry2):
             top = pl.multiple_of(k * 2 * NLAT, 2 * NLAT)
             zr, zi = z_ref[pl.ds(top, NLAT), :], z_ref[pl.ds(top + NLAT, NLAT), :]
             c, s = tw_ref[0], tw_ref[1]
@@ -424,22 +477,18 @@
             dr, di = wr[1] - wr[3], wi[1] - wi[3]
             vr = jnp.concatenate([ar + cr, br + di, ar - cr, br - di], axis=0)
             vi = jnp.concatenate([ai + ci, bi - dr, ai - ci, bi + dr], axis=0)
-            v = jnp.concatenate([vr, vi], axis=1).astype(BF16)
-
-            u = u_ref[k, n]
-            pre = dot(u, m1_ref[n], TN) + b1
-            sq = pre * pre
-            th = jnp.tanh(ROOT * pre * (1.0 + 0.044715 * sq))
-            act = (0.5 * pre * (1.0 + th)).astype(BF16)
-            slope = 0.5 * (1.0 + th) + 0.5 * pre * (1.0 - th * th) * (
-                ROOT * (1.0 + 3.0 * 0.044715 * sq)
-            )
-            d_pre = (dot(v, m2_ref[n], NT) * slope).astype(BF16)
-            g2_ref[...] += dot(act, v, TN)
-            g1_ref[...] += dot(u, d_pre)
-            bias_ref[0:1, :] += jnp.sum(d_pre.astype(F32), axis=0, keepdims=True)
-            bias_ref[1:2, :] += jnp.sum(v.astype(F32), axis=0, keepdims=True)
-            x = dot(d_pre, m1_ref[n], NT).astype(BF16).astype(F32)
+            here = pl.ds(pl.multiple_of(k * 256, 256), 256)
+            v_ref[here, :] = jnp.concatenate([vr, vi], axis=1).astype(BF16)
+            return carry2
+
+        lax.fori_loop(0, NK, radix, 0, unroll=True)
+        d_ref[...] = (dot(v_ref[...], m2_ref[n], NT) * slope_ref[n]).astype(BF16)
+        x_ref[...] = dot(d_ref[...], m1_ref[n], NT).astype(BF16).astype(F32)
+
+        def unradix(k, carry2):
+            top = pl.multiple_of(k * 2 * NLAT, 2 * NLAT)
+            c, s = tw_ref[0], tw_ref[1]
+            x = x_ref[pl.ds(pl.multiple_of(k * 256, 256), 256), :]
             xr = [x[j * NLAT : (j + 1) * NLAT, :BS] for j in range(4)]
             xi = [x[j * NLAT : (j + 1) * NLAT, BS:] for j in range(4)]
             ar, ai = xr[0] + xr[2], xi[0] + xi[2]
@@ -452,7 +501,12 @@
             e_ref[pl.ds(top + NLAT, NLAT), :] = (ei * c + er * s).astype(BF16)
             return carry2
 
-        lax.fori_loop(0, NK, mode, 0)
+        lax.fori_loop(0, NK, unradix, 0, unroll=True)
+
+        g1_ref[...] = dot(u_ref[n], d_ref[...])
+        g2_ref[...] = dot(act_ref[n], v_ref[...])
+        bias_ref[0:1, :] = jnp.sum(d_ref[...].astype(F32), axis=0, keepdims=True)
+        bias_ref[1:2, :] = jnp.sum(v_ref[...].astype(F32), axis=0, keepdims=True)
         for w, (grad, row) in enumerate(((g1_ref, 0), (g2_ref, 1))):
             full = grad[...]
             halves = (full[:BS, :BS] + full[BS:, BS:], full[:BS, BS:] - full[BS:, :BS])
@@ -467,30 +521,41 @@
             sumf.start(0)
 
         def inverse(j, carry2):
-            c = lax.rem(zed // 2 + 2 + j, 4)
-            where = pl.ds(pl.multiple_of(c * 256, 256), 256)
+            z = plane(j)
+            where = pl.ds(pl.multiple_of(z * 128, 128), 128)
             block = dot(inv_ref[where, :], e_ref[...]).astype(BF16)
-            b_ref[n, pl.ds(c * 16, 16)] = block.reshape(16, 16, PS)
-            home.start(n, c * 16, 16)
+            b_ref[n, pl.ds(z * 8, 8)] = block.reshape(8, 16, PS)
+            home.start(n, z)
             return carry2
 
-        lax.fori_loop(0, 4, inverse, 0)
+        lax.fori_loop(0, 2, inverse, 0)
 
         @pl.when(n == 0)
         def _():
-            sumc.wait(0)
-            sumc.start(1)
-
+            sumc.wait(1)
+            sumc.start(2)
+
+        @pl.when(n == 1)
+        def _():
+            sumc.wait(2)
+            sumc.start(3)
+            sumf.wait(0)
+            sumf.start(1)
+
+        lax.fori_loop(2, 4, inverse, 0)
+
+        @pl.when(n == 1)
+        def _():
+            sumf.wait(1)
+            sumf.start(2)
+
+        lax.fori_loop(4, 8, inverse, 0)
         return carry
 
     lax.fori_loop(0, 2, block_filter, 0)
-    sumc.wait(1)
-    sumc.start(2)
-    sumf.wait(0)
-    sumf.start(1)
-    sumc.wait(2)
-    sumc.start(3)
-    load(5).wait()
+    sumf.wait(2)
+    sumf.start(3)
+    load(4).wait()
 
     def synthesis(n):
         home.wait_recv(n)
@@ -506,10 +571,6 @@
                 r += size
 
     synthesis(0)
-    sumf.wait(1)
-    sumf.start(2)
-    sumf.wait(2)
-    sumf.start(3)
     synthesis(1)
     sumc.wait(3)
     sumf.wait(3)
@@ -523,6 +584,7 @@
         return carry
 
     lax.fori_loop(0, ROWS, gather_sent, 0)
+    hop(relay_ref, relay_ref, 11, LAST, (me, core)).wait_send()
 
 
 def fused(*args):
@@ -531,13 +593,15 @@
     half, wide = BF16, F32
     scratch = [
         ((ROWS, 3, CO, PAD), half), ((ROWS, CI, LON), half), ((3 * CI, 3 * CO), half),
-        ((NK, 2, CI, 256), half), ((16 * NLAT, PAD), half), ((16 * NLAT, PAD), half),
+        ((2, CI, NK * 256), half), ((16 * NLAT, PAD), half), ((16 * NLAT, PAD), half),
         ((NK * 2 * NLAT, 16 * NLAT), half), ((16 * NLAT, NK * 2 * NLAT), half),
         ((2, CI, CI), half), ((2, CI, CI), half),
         ((2, PS, PAD), wide), ((2, PS, PAD), half), ((3 * CI, 3 * CO), wide), ((3 * CI, PAD), half),
         ((2, NLAT, 16, PS), half), ((2, NLAT, 16, PS), half), ((2, NLAT, 16, PS), half),
         ((2, NLAT, 16, PS), half), ((NK * 2 * NLAT, PS), wide), ((NK * 2 * NLAT, PS), half),
         ((CI, CI), wide), ((CI, CI), wide), ((8, CI), wide), ((3, CI, PAD), wide),
+        ((64, PAD), half), ((2, CI, NK * 256), half), ((2, NK * 256, CI), wide),
+        ((NK * 256, CI), half), ((NK * 256, CI), half), ((NK * 256, CI), wide),
         ((8, QC, 128), half), ((8, QF, 128), half),
         ((8, QC, 128), half), ((8 * QCZ, 128), half), ((8, QCZ, 128), half), ((8 * QCZ, 128), half),
         ((8, QF, 128), half), ((8 * QFZ, 128), half), ((8, QFZ, 128), half), ((8 * QFZ, 128), half),
@@ -553,7 +617,7 @@
         out_specs=[vmem] * 3,
         scratch_shapes=[pltpu.VMEM(s, t) for s, t in scratch]
         + [
-            dma((6,)), dma((9,)), dma((11, ROWS)), dma((11, ROWS)),
+            pltpu.SemaphoreType.REGULAR, dma((5,)), dma((9,)), dma((2 * NK,)), dma((12, ROWS)), dma((12, ROWS)),
             dma((2, NLAT)), dma((2, NLAT)), dma((2, NLAT)), dma((2, NLAT)),
             dma((4, 8)), dma((4, 8)), dma((4, 8)), dma((4, 8)),
         ],
@@ -565,7 +629,8 @@
     )(*args)
 
 
-def unpack_kernel(c_ref, f_ref, gc_ref, w1_ref, b1_ref, w2_ref, b2_ref):
+def unpack_kernel(in_ref, c_ref, f_ref, out_ref, gc_ref, w1_ref, b1_ref, w2_ref, b2_ref):
+    out_ref[...] = in_ref[...]
     for rr in range(4):
         for cc in range(2):
             for t in range(3):
@@ -585,17 +650,18 @@
                 b_ref[n, part : part + 1, :] = block[BS : BS + 1, :BS]
 
 
-def unpack(sumc, sumf):
+def unpack(grad_in, sumc, sumf):
     vmem = pl.BlockSpec(memory_space=pltpu.VMEM)
     outs = [(3, 3, CI, CO), (2, 2, BS, BS), (2, 2, BS), (2, 2, BS, BS), (2, 2, BS)]
     return pl.pallas_call(
         unpack_kernel,
-        out_shape=[jax.ShapeDtypeStruct(s, F32) for s in outs],
-        in_specs=[vmem] * 2,
-        out_specs=[vmem] * 5,
+        out_shape=[jax.ShapeDtypeStruct((ROWS, CI, LON), BF16)]
+        + [jax.ShapeDtypeStruct(s, F32) for s in outs],
+        in_specs=[vmem] * 3,
+        out_specs=[vmem] * 6,
         compiler_params=pltpu.CompilerParams(vmem_limit_bytes=VMEM),
         name="lay_out",
-    )(sumc, sumf)
+    )(grad_in, sumc, sumf)
 
 
 def on_device(output_gradient, conv_in, conv_weight, modes, w1, b1, w2):
@@ -609,8 +675,8 @@
         jnp.transpose(modes, (0, 2, 3, 4, 1)).reshape(NK, 2, CI, 256),
         w1, b1, w2, tw, ana, syn, fwd, inv,
     )
-    grad_in = jnp.transpose(grad_in, (0, 2, 1))
-    return (grad_in, *unpack(sumc, sumf))
+    grad_in, *sums = unpack(grad_in, sumc, sumf)
+    return (jnp.transpose(grad_in, (0, 2, 1)), *sums)
 
 
 def solution(mesh):

time: 151 us -> 140 us (0.927)
  Pallas kernels: 146 us -> 137 us
  local copies, waits for them, and re-layouts: 2.67 us -> 0 us
    pallas_call x1, Pallas kernels: 144 us -> 134 us  [fused(): pl.pallas_call(fused_kernel, out_shape=[jax.ShapeDtypeStruct((ROWS, CI, L...]
    unnamed x1 -> x0, local copies, waits for them, and re-layouts: 2.67 us -> none
where the time goes in v3:
time: 140 us; the launch traced here: 138 us
  Pallas kernels  137 us (98%)
    pallas_call x1, Pallas kernels, fused(): pl.pallas_call(fused_kernel, out_shape=[jax.ShapeDtypeStruct((ROWS, CI, L...  134 us
    pallas_call x1, Pallas kernels, unpack(): pl.pallas_call(unpack_kernel, out_shape=[jax.ShapeDtypeStruct((ROWS, CI,...  3.68 us

profile of v3, /device:TPU:8, one launch (start us, length us, event | category | flops | bytes accessed | tf_op | source)
XLA Modules:
  0.0 137.9 jit_solution(900477484875356290)
XLA Ops:
  0.6 133.5 %block_backward.1 = (bf16[4,192,900]{2,1,0:T(8,128)(2,1)}, bf16[8,432,128]{2,1,0:T(8,128)(2,1)}, bf16[8,112,128]{2,1,0:T(8,128)(2,1)}) custom-call(bf16[4,64,900]{2,1,0:T(8,128)(2,1)} %bitcast.9, bf16[4,192,900]{2,1,0:T(8,128)(2,1)} %bitcast.6, bf16[3,3,192,256]{3,2,1,0:T(8,128)(2,1)} %cw_hbm.1, bf16[7,2,192,256]{3,2,1,0:T(8,128)(2,1)} %bitcast.8, ...), custom_call_target="tpu_custom_call" | custom-call | flops 16000000000 | bytes 33554432 | tf_op jit(solution)/shard_map/block_backward/pallas_call | solution.py:609
  134.2 3.7 %lay_out.1 = (bf16[4,192,900]{2,1,0:T(8,128)(2,1)}, f32[3,3,192,256]{3,2,1,0:T(8,128)}, f32[2,2,96,96]{3,2,1,0:T(8,128)}, f32[2,2,96]{2,1,0:T(2,128)}, f32[2,2,96,96]{3,2,1,0:T(8,128)}, /*index=5*/f32[2,2,96]{2,1,0:T(2,128)}) custom-call(bf16[4,192,900]{2,1,0:T(8,128)(2,1)} %get-tuple-element.15.in_ref, bf16[8,432,128]{2,1,0:T(8,128)(2,1)} %get-tuple-element.16.c_ref, ...), custom_call_target="tpu_custom_call" | custom-call | tf_op jit(solution)/shard_map/lay_out/pallas_call | solution.py:656

commit v4 on v3

--- a/solution.py
+++ b/solution.py
@@ -252,8 +252,6 @@
                     wloads.at[a * 3 + b],
                 )
             )
-    for copy in wcopies:
-        copy.start()
     ucopies = []
     for n in range(2):
         for k in range(NK):
@@ -262,11 +260,6 @@
                     u_hbm.at[k, n], u_ref.at[n, :, pl.ds(k * 256, 256)], uloads.at[n * NK + k]
                 )
             )
-    for copy in ucopies:
-        copy.start()
-    for i in range(5):
-        load(i).start()
-
     def rows(c):
         return pl.ds(pl.multiple_of(c * 64, 64), 64)
 
@@ -314,6 +307,12 @@
         go(at(p, 1, ch), at(p, 1, ch), 5, p, (me, core))
 
     lax.fori_loop(1, 8, plane_here, 0)
+    for copy in wcopies:
+        copy.start()
+    for copy in ucopies:
+        copy.start()
+    for i in range(5):
+        load(i).start()
 
     for w, m_ref in ((w1_ref, m1_ref), (w2_ref, m2_ref)):
         for n in range(2):
@@ -539,22 +538,18 @@
         def _():
             sumc.wait(2)
             sumc.start(3)
+
+        lax.fori_loop(2, 4, inverse, 0)
+
+        @pl.when(n == 1)
+        def _():
             sumf.wait(0)
             sumf.start(1)
 
-        lax.fori_loop(2, 4, inverse, 0)
-
-        @pl.when(n == 1)
-        def _():
-            sumf.wait(1)
-            sumf.start(2)
-
         lax.fori_loop(4, 8, inverse, 0)
         return carry
 
     lax.fori_loop(0, 2, block_filter, 0)
-    sumf.wait(2)
-    sumf.start(3)
     load(4).wait()
 
     def synthesis(n):
@@ -570,7 +565,11 @@
                 out_ref[p, n * BS + s : n * BS + s + size, :] = part[r : r + size]
                 r += size
 
+    sumf.wait(1)
+    sumf.start(2)
     synthesis(0)
+    sumf.wait(2)
+    sumf.start(3)
     synthesis(1)
     sumc.wait(3)
     sumf.wait(3)
@@ -629,8 +628,17 @@
     )(*args)
 
 
-def unpack_kernel(in_ref, c_ref, f_ref, out_ref, gc_ref, w1_ref, b1_ref, w2_ref, b2_ref):
-    out_ref[...] = in_ref[...]
+def unpack_kernel(
+    in_hbm, c_ref, f_ref, out_hbm, gc_ref, w1_ref, b1_ref, w2_ref, b2_ref, rows_ref, taken, given
+):
+    take = [
+        pltpu.make_async_copy(in_hbm.at[p], rows_ref.at[p], taken.at[p]) for p in range(ROWS)
+    ]
+    give = [
+        pltpu.make_async_copy(rows_ref.at[p], out_hbm.at[p], given.at[p]) for p in range(ROWS)
+    ]
+    for move in take:
+        move.start()
     for rr in range(4):
         for cc in range(2):
             for t in range(3):
@@ -642,23 +650,33 @@
                     at = t * 144 + r - rr * 144
                     gc_ref[a, b, c : c + n, o : o + 128] = c_ref[rr * 2 + cc, at : at + n, :].astype(F32)
                     r += n
+    for p in range(ROWS):
+        take[p].wait()
+        give[p].start()
     for w, (w_ref, b_ref) in enumerate(((w1_ref, b1_ref), (w2_ref, b2_ref))):
         for n in range(2):
             for part in range(2):
                 block = f_ref[w * 4 + n * 2 + part].astype(F32)
                 w_ref[n, part] = block[:BS, :BS]
                 b_ref[n, part : part + 1, :] = block[BS : BS + 1, :BS]
+    for move in give:
+        move.wait()
 
 
 def unpack(grad_in, sumc, sumf):
-    vmem = pl.BlockSpec(memory_space=pltpu.VMEM)
+    vmem, anywhere = pl.BlockSpec(memory_space=pltpu.VMEM), pl.BlockSpec(memory_space=pl.ANY)
     outs = [(3, 3, CI, CO), (2, 2, BS, BS), (2, 2, BS), (2, 2, BS, BS), (2, 2, BS)]
     return pl.pallas_call(
         unpack_kernel,
         out_shape=[jax.ShapeDtypeStruct((ROWS, CI, LON), BF16)]
         + [jax.ShapeDtypeStruct(s, F32) for s in outs],
-        in_specs=[vmem] * 3,
-        out_specs=[vmem] * 6,
+        in_specs=[anywhere] + [vmem] * 2,
+        out_specs=[anywhere] + [vmem] * 5,
+        scratch_shapes=[
+            pltpu.VMEM((ROWS, CI, LON), BF16),
+            pltpu.SemaphoreType.DMA((ROWS,)),
+            pltpu.SemaphoreType.DMA((ROWS,)),
+        ],
         compiler_params=pltpu.CompilerParams(vmem_limit_bytes=VMEM),
         name="lay_out",
     )(grad_in, sumc, sumf)

time: 140 us -> 143 us (1.021)
  Pallas kernels: 137 us -> 141 us
    pallas_call x1, Pallas kernels: 134 us -> 136 us  [fused(): pl.pallas_call(fused_kernel, out_shape=[jax.ShapeDtypeStruct((ROWS, CI, L...]
where the time goes in v4:
time: 143 us; the launch traced here: 142 us
  Pallas kernels  141 us (99%)
    pallas_call x1, Pallas kernels, fused(): pl.pallas_call(fused_kernel, out_shape=[jax.ShapeDtypeStruct((ROWS, CI, L...  136 us
    pallas_call x1, Pallas kernels, unpack(): pl.pallas_call(unpack_kernel, out_shape=[jax.ShapeDtypeStruct((ROWS, CI,...  4.74 us

profile of v4, /device:TPU:8, one launch (start us, length us, event | category | flops | bytes accessed | tf_op | source)
XLA Modules:
  0.0 141.5 jit_solution(634458279919840671)
XLA Ops:
  0.6 136.1 %block_backward.1 = (bf16[4,192,900]{2,1,0:T(8,128)(2,1)}, bf16[8,432,128]{2,1,0:T(8,128)(2,1)}, bf16[8,112,128]{2,1,0:T(8,128)(2,1)}) custom-call(bf16[4,64,900]{2,1,0:T(8,128)(2,1)} %bitcast.9, bf16[4,192,900]{2,1,0:T(8,128)(2,1)} %bitcast.6, bf16[3,3,192,256]{3,2,1,0:T(8,128)(2,1)} %cw_hbm.1, bf16[7,2,192,256]{3,2,1,0:T(8,128)(2,1)} %bitcast.8, ...), custom_call_target="tpu_custom_call" | custom-call | flops 16000000000 | bytes 33554432 | tf_op jit(solution)/shard_map/block_backward/pallas_call | solution.py:608
  136.8 4.7 %lay_out.1 = (bf16[4,192,900]{2,1,0:T(8,128)(2,1)}, f32[3,3,192,256]{3,2,1,0:T(8,128)}, f32[2,2,96,96]{3,2,1,0:T(8,128)}, f32[2,2,96]{2,1,0:T(2,128)}, f32[2,2,96,96]{3,2,1,0:T(8,128)}, /*index=5*/f32[2,2,96]{2,1,0:T(2,128)}) custom-call(bf16[4,192,900]{2,1,0:T(8,128)(2,1)} %get-tuple-element.15.in_hbm, bf16[8,432,128]{2,1,0:T(8,128)(2,1)} %get-tuple-element.16.c_ref, ...), custom_call_target="tpu_custom_call" | custom-call | tf_op jit(solution)/shard_map/lay_out/pallas_call | solution.py:669
